TPU v7x, 512 devices: a whole 4x8x8 slice. The times are simulated.
512 devices in a mesh: dp: 8 (over y_lo, core), tensor: 32 (over z, x), section: 2 (over y_hi).
Axes of the slice: x: 4, y: 8 (y_hi: 2, y_lo: 4; y = y_hi * 4 + y_lo), z: 8, core: 2. Of those that a mesh axis runs over, the one named last changes fastest.
Arguments:
- structure_trunk_gradient: bfloat16 [6144, 10240], P(('dp', 'tensor', 'section')), may hold values from -6 to 6
- context: bfloat16 [6144, 5120], P(('dp', 'section'), 'tensor'), may hold values from -6 to 6
- residual: bfloat16 [6144, 10240], P(('dp', 'section'), 'tensor'), may hold values from -16 to 16
- gain: bfloat16 [10240], P('tensor'), may hold values from 0.5 to 1.5
- codes: bfloat16 [5120, 10240], P(None, 'tensor'), may hold values from -0.15625 to 0.15625
- exponents: int32 [40, 160], P(None, 'tensor'), may hold values from -3 to 1
- adapter_down_factor: bfloat16 [5120, 16], P('tensor'), may hold values from -0.078125 to 0.078125
- adapter_up_factor: bfloat16 [16, 10240], P(None, 'tensor'), may hold values from -1.5 to 1.5
- token_residue_map: int32 [16, 384], P(('dp', 'section')), may hold values from 0 to 383, each once within a row
- lengths: int32 [16], P(('dp', 'section')), may hold values from 192 to 384, as said below
Outputs:
- context_gradient: bfloat16 [5120, 6144], P('tensor', ('dp', 'section'))
- hidden_gradient: bfloat16 [6144, 10240], P(('dp', 'section'), 'tensor')
- down_factor_gradient: float32 [5120, 16], P('tensor')
- up_factor_gradient: float32 [16, 10240], P(None, 'tensor')
- final_hidden: bfloat16 [6144, 10240], P(('dp', 'section'), 'tensor')
Inputs may be any that keep to these rules, and one draw needn't show every extreme that they name: `token_residue_map`: each row is a permutation of 0 to 383. `lengths`: one crop has 384 valid tokens and one has 192.
All inputs are finite; a program needn't handle non-finite values.
Results may differ from a plain program's by a relative error of at most 0.015.
Values may be sent and summed in bfloat16 or wider, within the bound.
A program may use at most 64 MiB of HBM per device.

v0:
```python
import jax
import jax.numpy as jnp
from jax import lax
from jax.sharding import PartitionSpec as P

MODEL_WIDTH = 10240


ADAPTER_SCALE = 2.0


def dequantize(codes, exponents):
    block_rows = codes.shape[0] // exponents.shape[0]
    block_cols = codes.shape[1] // exponents.shape[1]
    factor = jnp.exp2(exponents.astype(jnp.float32))
    spread = codes.astype(jnp.float32).reshape(
        exponents.shape[0], block_rows, exponents.shape[1], block_cols
    )
    return (spread * factor[:, None, :, None]).reshape(codes.shape).astype(jnp.bfloat16)


def on_device(
    structure_trunk_gradient,
    context,
    residual,
    gain,
    codes,
    exponents,
    adapter_down_factor,
    adapter_up_factor,
    token_residue_map,
    lengths,
):
    tensor_count = lax.axis_size("tensor")
    owner_rows = structure_trunk_gradient.shape[0]
    crop_rows = context.shape[0]
    residue = token_residue_map[0]
    spread_rows = lax.all_to_all(
        structure_trunk_gradient, "tensor", split_axis=1, concat_axis=0, tiled=True
    )
    relaid = lax.all_gather(spread_rows, "section", axis=0, tiled=True)
    global_row = lax.axis_index("section") * crop_rows + residue
    owner_index = global_row // owner_rows
    source_row = (
        owner_index % 2 * (tensor_count * owner_rows)
        + owner_index // 2 * owner_rows
        + global_row % owner_rows
    )
    picked = jnp.take(relaid, source_row, axis=0)
    positions = lax.broadcasted_iota(jnp.int32, (crop_rows, 1), 0)
    upstream = jnp.where(positions < lengths[0], picked.astype(jnp.float32), 0.0)
    weights = dequantize(codes, exponents)
    projected_output = jnp.dot(
        lax.all_gather(context, "tensor", axis=1, tiled=True),
        weights,
        preferred_element_type=jnp.float32,
    )
    inner_product_sum = lax.psum(
        jnp.dot(context, adapter_down_factor, preferred_element_type=jnp.float32), "tensor"
    )
    inner_product = inner_product_sum.astype(jnp.bfloat16)
    hidden_state = projected_output + ADAPTER_SCALE * jnp.dot(
        inner_product, adapter_up_factor, preferred_element_type=jnp.float32
    )
    hidden_state = hidden_state + residual.astype(jnp.float32)
    row_total, row_squares = lax.psum(
        (jnp.sum(hidden_state, axis=1), jnp.sum(hidden_state * hidden_state, axis=1)), "tensor"
    )
    average = row_total / MODEL_WIDTH
    variance = row_squares / MODEL_WIDTH - average * average
    inverse = lax.rsqrt(variance + 1e-05)
    normed = (hidden_state - average[:, None]) * inverse[:, None]
    gain_values = gain.astype(jnp.float32)[None, :]
    final_hidden = (gain_values * normed).astype(jnp.bfloat16)
    scaled = gain_values * upstream
    scaled_total, scaled_dot = lax.psum(
        (jnp.sum(scaled, axis=1), jnp.sum(scaled * normed, axis=1)), "tensor"
    )
    first_mean = scaled_total / MODEL_WIDTH
    second_mean = scaled_dot / MODEL_WIDTH
    hidden_gradient = (
        inverse[:, None] * (scaled - first_mean[:, None] - normed * second_mean[:, None])
    ).astype(jnp.bfloat16)
    contract_product = (((1,), (1,)), ((), ()))
    passthrough_term = lax.dot_general(
        hidden_gradient, adapter_up_factor, contract_product, preferred_element_type=jnp.float32
    )
    passed_through = lax.psum(passthrough_term, "tensor").astype(jnp.bfloat16)
    head_rows = weights.shape[0] // tensor_count
    whole_term = lax.dot_general(
        weights, hidden_gradient, contract_product, preferred_element_type=jnp.float32
    )
    summed = lax.psum(whole_term.astype(jnp.bfloat16), "tensor").astype(jnp.float32)
    local_rows = lax.dynamic_slice_in_dim(
        summed, lax.axis_index("tensor") * head_rows, head_rows, 0
    )
    adapter_term = lax.dot_general(
        adapter_down_factor, passed_through, contract_product, preferred_element_type=jnp.float32
    )
    context_gradient = (local_rows + ADAPTER_SCALE * adapter_term).astype(jnp.bfloat16)
    row_contraction = (((0,), (0,)), ((), ()))
    down_factor_gradient = ADAPTER_SCALE * lax.dot_general(
        context, passed_through, row_contraction, preferred_element_type=jnp.float32
    )
    up_factor_gradient = ADAPTER_SCALE * lax.dot_general(
        inner_product, hidden_gradient, row_contraction, preferred_element_type=jnp.float32
    )
    down_factor_gradient, up_factor_gradient = lax.psum(
        (down_factor_gradient, up_factor_gradient), ("dp", "section")
    )
    return (
        context_gradient,
        hidden_gradient,
        down_factor_gradient,
        up_factor_gradient,
        final_hidden,
    )


def solution(mesh):
    in_specs = (
        P(("dp", "tensor", "section"), None),
        P(("dp", "section"), "tensor"),
        P(("dp", "section"), "tensor"),
        P("tensor"),
        P(None, "tensor"),
        P(None, "tensor"),
        P("tensor", None),
        P(None, "tensor"),
        P(("dp", "section"), None),
        P(("dp", "section")),
    )
    out_specs = (
        P("tensor", ("dp", "section")),
        P(("dp", "section"), "tensor"),
        P("tensor", None),
        P(None, "tensor"),
        P(("dp", "section"), "tensor"),
    )
    return jax.shard_map(
        on_device, mesh=mesh, in_specs=in_specs, out_specs=out_specs, check_vma=False
    )
```

profile of v0, /device:TPU:6, one launch (start us, length us, event | category | flops | bytes accessed | tf_op | source)
XLA Modules:
  0.0 571.3 jit_solution(5710609956390365390)
XLA Ops:
  7.2 0.0 copy-start
  7.2 0.0 all-gather.2.cloned.1.call-start
  7.2 0.7 all-gather.2.cloned.1.call-update
  7.9 1.3 all_to_all.14
  9.3 0.8 copy.17
  10.1 13.4 %all-to-all-start = ((bf16[12,32,320]{2,0,1:T(8,128)(2,1)}), bf16[12,32,320]{2,0,1:T(8,128)(2,1)S(1)}, u32[]{:S(2)}, u32[]{:S(2)}) async-start(bf16[12,32,320]{2,0,1:T(8,128)(2,1)} %copy.17), calls=%async_computation | async-start | bytes 786432 | tf_op jit(solution)/shard_map/all_to_all | solution.py:38
  23.5 0.0 all-reduce.5.cloned.1.call-start
  23.6 0.7 compare_reduce_fusion
  24.3 0.7 fusion.25
  25.0 0.7 fusion.20
  25.7 1.0 fusion.26
  26.8 0.7 convert_element_type.44
  28.1 133.8 %psum.63 = bf16[384,16]{0,1:T(8,128)(2,1)S(1)} all-reduce(f32[384,16]{0,1:T(8,128)S(1)} %fusion.26), channel_id=1, replica_groups=mesh['dp'=8,'tensor'=32,'section'=2] {'tensor'}, use_global_device_ids=true, to_apply=%region_0.1 | all-reduce | flops 6144 | bytes 36864 | tf_op jit(solution)/shard_map/psum | solution.py:58
  161.9 0.6 iota_compare_fusion
  162.5 0.7 multiply_exponential_fusion
  163.2 0.0 all-to-all-done
  163.2 0.1 all_to_all.17
  163.3 13.8 %all_gather.7 = bf16[768,320]{1,0:T(8,128)(2,1)S(1)} all-gather(bf16[384,320]{1,0:T(8,128)(2,1)S(1)} %all_to_all.17), channel_id=1, replica_groups=mesh['dp'=8,'tensor'=32,'section'=2] {'section'}, dimensions={0}, use_global_device_ids=true | all-gather | bytes 737280 | tf_op jit(solution)/shard_map/all_gather | solution.py:41
  177.1 2.5 gather_fusion
  179.7 1.3 copy.18
  181.0 0.0 copy-start.4
  181.0 0.0 all-gather.2.cloned.1.call-done
  181.0 0.5 mul.126
  181.5 0.0 copy-start.1
  181.5 0.2 copy-done.2
  181.7 6.2 %convolution_bitcast_fusion = f32[384,320]{0,1:T(8,128)S(1)} fusion(bf16[384,5120]{0,1:T(8,128)(2,1)} %all-gather.2.cloned.1.call-done, f32[40,8,40,128]{3,2,1,0:T(8,128)S(1)} %bitcast.58, bf16[5120,320]{0,1:T(8,128)(2,1)S(1)} %copy-done.2), kind=kOutput, calls=%fused_computation.5 | convolution fusion | flops 1263206400 | bytes 14254080 | tf_op jit(solution)/shard_map/dot_general | solution.py:53
  187.9 0.0 copy-done.1
  187.9 0.0 copy-done
  188.0 0.0 copy-done.6
  188.0 1.7 multiply_reduce_fusion.1
  189.6 75.9 %all-reduce.1 = (f32[384]{0:T(512)}, f32[384]{0:T(512)}) all-reduce(f32[384]{0:T(512)S(1)} %get-tuple-element.5, f32[384]{0:T(512)} %get-tuple-element.6), channel_id=1, replica_groups=mesh['dp'=8,'tensor'=32,'section'=2] {'tensor'}, use_global_device_ids=true, to_apply=%region_2.3 | all-reduce | flops 768 | bytes 6144 | tf_op jit(solution)/shard_map/psum | solution.py:66
  265.5 0.7 broadcast_multiply_fusion.2
  266.2 0.0 copy-done.4
  266.2 2.5 fusion.7
  268.7 0.0 copy-done.8
  268.8 69.7 %all-reduce = (f32[384]{0:T(512)S(1)}, f32[384]{0:T(512)S(1)}) all-reduce(f32[384]{0:T(512)} %get-tuple-element.8, f32[384]{0:T(512)} %get-tuple-element.7), channel_id=1, replica_groups=mesh['dp'=8,'tensor'=32,'section'=2] {'tensor'}, use_global_device_ids=true, to_apply=%region_8.9 | all-reduce | flops 768 | bytes 6144 | tf_op jit(solution)/shard_map/psum | solution.py:76
  338.5 1.4 multiply_convert_fusion.1
  339.9 0.0 copy-start.3
  339.9 8.2 %convolution_convert_fusion = bf16[5120,384]{1,0:T(8,128)(2,1)} fusion(bf16[384,320]{0,1:T(8,128)(2,1)S(1)} %multiply_convert_fusion.1, f32[40,8,40,128]{3,2,1,0:T(8,128)} %bitcast.59, bf16[5120,320]{0,1:T(8,128)(2,1)S(1)} %copy-done.2), kind=kOutput, calls=%fused_computation.1 | convolution fusion | flops 1265172480 | bytes 14008320 | tf_op jit(solution)/shard_map/dot_general | solution.py:90
  348.0 0.0 all-reduce.5.cloned.1.call-update
  348.1 0.1 fusion.27
  348.2 136.7 %psum.69 = bf16[384,16]{0,1:T(8,128)(2,1)S(1)} all-reduce(f32[384,16]{0,1:T(8,128)S(1)} %fusion.27), channel_id=1, replica_groups=mesh['dp'=8,'tensor'=32,'section'=2] {'tensor'}, use_global_device_ids=true, to_apply=%region_10.11 | all-reduce | flops 6144 | bytes 36864 | tf_op jit(solution)/shard_map/psum | solution.py:88
  484.9 0.0 copy-done.5
  484.9 0.1 fusion.6
  485.1 0.0 copy-done.3
  485.1 0.1 convolution_multiply_fusion.2
  485.2 77.4 %all-reduce.2 = (f32[160,16]{0,1:T(8,128)}, f32[16,320]{1,0:T(8,128)}) all-reduce(f32[160,16]{0,1:T(8,128)S(1)} %fusion.6, f32[16,320]{1,0:T(8,128)S(1)} %convolution_multiply_fusion.2), channel_id=1, replica_groups=mesh['dp'=8,'tensor'=32,'section'=2] {'dp','section'}, use_global_device_ids=true, to_apply=%region_11.12 | all-reduce | flops 7680 | bytes 61440 | tf_op jit(solution)/shard_map/psum | solution.py:108
  562.7 1.8 fusion.5
  (10 shorter events, 0.0 us)
Async XLA Ops:
  7.2 180.8 %copy-start = (bf16[16,320]{1,0:T(8,128)(2,1)S(1)}, bf16[16,320]{1,0:T(8,128)(2,1)}, u32[]{:S(2)}) copy-start(bf16[16,320]{1,0:T(8,128)(2,1)} %param.17) | copy-start | bytes 30724
  7.2 173.8 %all-gather.2.cloned.1.call-start = ((), (), s32[]{:S(2)}) async-start(), calls=%async_computation.1 | async-start | bytes 4055040 | tf_op jit(solution)/shard_map/all_gather | solution.py:54
  10.1 153.1 %all-to-all-start = ((bf16[12,32,320]{2,0,1:T(8,128)(2,1)}), bf16[12,32,320]{2,0,1:T(8,128)(2,1)S(1)}, u32[]{:S(2)}, u32[]{:S(2)}) async-start(bf16[12,32,320]{2,0,1:T(8,128)(2,1)} %copy.17), calls=%async_computation | async-start | bytes 786432 | tf_op jit(solution)/shard_map/all_to_all | solution.py:38
  23.5 539.2 %all-reduce.5.cloned.1.call-start = ((), (), s32[]{:S(2)}) async-start(), calls=%async_computation.2 | async-start | bytes 7864320 | tf_op jit(solution)/shard_map/psum | solution.py:93
  179.7 2.0 copy-start.2
  181.0 85.3 %copy-start.4 = (bf16[384,320]{0,1:T(8,128)(2,1)}, bf16[384,320]{0,1:T(8,128)(2,1)S(1)}, u32[]{:S(2)}) copy-start(bf16[384,320]{0,1:T(8,128)(2,1)S(1)} %copy.18) | copy-start | bytes 737284
  181.5 6.4 %copy-start.1 = (f32[40,128,5,64]{1,0,3,2:T(8,128)}, f32[40,128,5,64]{1,0,3,2:T(8,128)S(1)}, u32[]{:S(2)}) copy-start(f32[40,128,5,64]{1,0,3,2:T(8,128)S(1)} %mul.126) | copy-start | bytes 19660804
  181.7 6.3 %copy-start.6 = (bf16[384,320]{0,1:T(8,128)(2,1)S(1)}, bf16[384,320]{0,1:T(8,128)(2,1)}, u32[]{:S(2)}) copy-start(bf16[384,320]{0,1:T(8,128)(2,1)} %param.12) | copy-start | bytes 737284
  266.2 2.5 copy-start.8
  339.9 145.2 %copy-start.3 = (bf16[384,320]{0,1:T(8,128)(2,1)}, bf16[384,320]{0,1:T(8,128)(2,1)S(1)}, u32[]{:S(2)}) copy-start(bf16[384,320]{0,1:T(8,128)(2,1)S(1)} %multiply_convert_fusion.1) | copy-start | bytes 737284
  348.0 136.9 %copy-start.5 = (bf16[384,160]{0,1:T(8,128)(2,1)S(1)}, bf16[384,160]{0,1:T(8,128)(2,1)}, u32[]{:S(2)}) copy-start(bf16[384,160]{0,1:T(8,128)(2,1)} %param.11) | copy-start | bytes 368644
  348.0 214.6 %copy-start.7 = (bf16[160,16]{0,1:T(8,128)(2,1)S(1)}, bf16[160,16]{0,1:T(8,128)(2,1)}, u32[]{:S(2)}) copy-start(bf16[160,16]{0,1:T(8,128)(2,1)} %param.16) | copy-start | bytes 15364
Sparse Core Ops, SparseCore 0:
  11.2 90.3 all-gather.1
  348.2 174.6 all-reduce.4
where the time goes:
time: 583 us; the launch traced here: 571 us
  blocking collectives  507 us (87%)
  matrix products  19.3 us (3%)
  between operations  14.8 us (3%)
  starting transfers between devices  13.5 us (2%)
  other arithmetic  8.67 us (1%)
  local copies, waits for them, and re-layouts  6.84 us (1%)
    psum x1, blocking collectives, on_device(): passed_through = lax.psum(passthrough_term, 'tensor').astype(jnp.bfloat16)  137 us
    psum x1, blocking collectives, on_device(): lax.psum(jnp.dot(context, adapter_down_factor, preferred_element_type=jnp...  134 us
    psum x1, blocking collectives, on_device(): lax.psum((down_factor_gradient, up_factor_gradient), ('dp', 'section'))  77.4 us
    psum x1, blocking collectives, on_device(): lax.psum((jnp.sum(hidden_state, axis=1), jnp.sum(hidden_state * hidden_st...  75.9 us
    psum x1, blocking collectives, on_device(): lax.psum((jnp.sum(scaled, axis=1), jnp.sum(scaled * normed, axis=1)), 'te...  69.7 us
    all_gather x1, blocking collectives, on_device(): relaid = lax.all_gather(spread_rows, 'section', axis=0, tiled=True)  13.8 us
    all_to_all x1, starting transfers between devices, on_device(): lax.all_to_all(structure_trunk_gradient, 'tensor', split_axis=1, concat_a...  13.4 us
  transfers between devices with their start and end apart: 3, of which 0 were waited for; matrix products, arithmetic and copies ran while one was open for 2% of the time, Pallas kernels for 0%

commit v1 on v0

v1 whole, which is shorter than its diff:
```python
import functools

import jax
import jax.numpy as jnp
from jax import lax
from jax.experimental import pallas as pl
from jax.experimental.pallas import tpu as pltpu
from jax.sharding import PartitionSpec as P

MODEL_WIDTH = 10240
DIMS = 5120
ADAPTER_SCALE = 2.0
CROP = 384
COLS = 320
ROWS = 160
RANK = 16
NX = 4
NZ = 8
NY = 8
BLKR = 128
BLKC = 64
OWNED = 12
SLOT = 16
F32 = jnp.float32
BF16 = jnp.bfloat16
MESH = pl.DeviceIdType.MESH
QR = 96
PR = 80
CR = QR + PR
TOKEN_BLOCK = 128
NBLOCK = CROP // TOKEN_BLOCK

SENDS = 200


def dot(a, b, dims=((1,), (0,))):
    return lax.dot_general(a, b, (dims, ((), ())), preferred_element_type=F32)


def kernel(
    grad_ref, ctx_ref, res_ref, gain_ref, codes_ref, exp_ref, down_ref, up_ref, map_ref, len_ref,
    cg_ref, hg_ref, dg_ref, ug_ref, fh_ref,
    W, C, WT, WX, GM, GR, ACC, RT, HX, PART, RS, RR, LR, UP4, ST, SX, SZ, TH, TZ, GA, GC, GY, GS,
    send_sem, recv_sem, load_sem, gsend_sem, grecv_sem,
):
    dp = lax.axis_index("dp")
    t = lax.axis_index("tensor")
    sec = lax.axis_index("section")
    x = lax.rem(t, NX)
    z = lax.div(t, NX)
    core = lax.rem(dp, 2)
    y = sec * (NY // 2) + lax.div(dp, 2)

    def dev_x(r):
        return (dp, z * NX + lax.rem(x + r, NX), sec)

    def dev_z(r):
        return (dp, lax.rem(z + r, NZ) * NX + x, sec)

    def dev_y(r):
        other = lax.rem(y + r, NY)
        return (lax.rem(other, NY // 2) * 2 + core, t, lax.div(other, NY // 2))

    other_core = (dp + 1 - 2 * core, t, sec)
    target_sec = lax.div(t, 16)
    self_target = (target_sec == sec).astype(jnp.int32)

    def w_rows(index):
        return pl.ds(pl.multiple_of(index * ROWS, 32), ROWS)

    load = pltpu.make_async_copy(codes_ref, W, load_sem)
    load.start()

    barrier = pltpu.get_barrier_semaphore()

    def greet(device):
        pl.semaphore_signal(barrier, inc=1, device_id=device, device_id_type=MESH)

    for r in range(1, NX):
        greet(dev_x(r))
    for r in range(1, NZ):
        greet(dev_z(r))
    for r in range(1, NY):
        greet(dev_y(r))
    greet(other_core)

    @pl.loop(0, 32)
    def _(i):
        src_t = sec * 16 + lax.div(i, 2)
        src_s = lax.rem(i, 2)

        @pl.when(jnp.logical_or(src_t != t, src_s != sec))
        def _():
            greet((dp, src_t, src_s))

    counter = [0]

    def copy(src, dst, device):
        k = counter[0]
        counter[0] += 1
        return pltpu.make_async_remote_copy(
            src_ref=src, dst_ref=dst, send_sem=send_sem.at[k], recv_sem=recv_sem.at[k],
            device_id=device, device_id_type=MESH,
        )

    pending = []

    def start(c):
        c.start()
        pending.append(c)
        return c

    C[0, 0:ROWS, :] = ctx_ref[...].astype(F32).T.astype(BF16)
    C[0, ROWS:CR, :] = jnp.zeros((RANK, CROP), BF16)
    C[0, ROWS:CR, 0:ROWS] = down_ref[...].astype(F32).T.astype(BF16)
    UP4[0] = up_ref[...]
    GM[...] = jnp.zeros_like(GM)
    for i in range(32):
        GM[i, 0:OWNED, :] = grad_ref[:, i * COLS : (i + 1) * COLS]

    pl.semaphore_wait(barrier, (NX - 1) + (NZ - 1) + (NY - 1) + 1 + 32 - self_target)

    def q_rows(slot):
        return C.at[slot, 0:QR]

    def p_rows(rz):
        return C.at[pl.ds(rz * NX, NX), QR:CR]

    def z_ring_q(step):
        if step < 4:
            right = copy(q_rows(((NZ - step + 1) % NZ) * NX), q_rows((NZ - step) * NX), dev_z(1))
            left = copy(q_rows((step - 1) * NX), q_rows(step * NX), dev_z(NZ - 1))
        else:
            right = copy(C.at[5 * NX, 0:48], C.at[4 * NX, 0:48], dev_z(1))
            left = copy(C.at[3 * NX, 48:QR], C.at[4 * NX, 48:QR], dev_z(NZ - 1))
        return start(right), start(left)

    def z_ring_p(step):
        if step < 4:
            right = copy(p_rows((NZ - step + 1) % NZ), p_rows(NZ - step), dev_z(1))
            left = copy(p_rows(step - 1), p_rows(step), dev_z(NZ - 1))
        else:
            right = copy(C.at[5 * NX : 6 * NX, QR : QR + 48], C.at[4 * NX : 5 * NX, QR : QR + 48], dev_z(1))
            left = copy(C.at[3 * NX : 4 * NX, QR + 48 : CR], C.at[4 * NX : 5 * NX, QR + 48 : CR], dev_z(NZ - 1))
        return start(right), start(left)

    def x_first(rz, lo, hi):
        b = rz * NX
        right = copy(C.at[b, lo:hi], C.at[b + 3, lo:hi], dev_x(1))
        left = copy(C.at[b, lo:hi], C.at[b + 1, lo:hi], dev_x(NX - 1))
        return start(right), start(left)

    def x_second(rz, lo, mid, hi):
        b = rz * NX
        right = copy(C.at[b + 3, lo:mid], C.at[b + 2, lo:mid], dev_x(1))
        left = copy(C.at[b + 1, mid:hi], C.at[b + 2, mid:hi], dev_x(NX - 1))
        return start(right), start(left)

    def arrived(pair):
        for c in pair:
            c.wait_recv()

    qz1 = z_ring_q(1)
    px1 = x_first(0, QR, CR)
    qx1 = {0: x_first(0, 0, QR)}
    qx2 = {}
    upc = [start(copy(UP4.at[0], UP4.at[NX - r], dev_x(r))) for r in range(1, NX)]

    my_slot = lax.rem(t, 16) * 2 + sec

    def grad_copy(to):
        return pltpu.make_async_remote_copy(
            src_ref=GM.at[to], dst_ref=GR.at[my_slot], send_sem=gsend_sem, recv_sem=grecv_sem,
            device_id=(dp, to, target_sec), device_id_type=MESH,
        )

    local = pltpu.make_async_copy(GM.at[t], GR.at[my_slot], grecv_sem)

    @pl.when(self_target == 1)
    def _():
        local.start()

    @pl.when(self_target == 0)
    def _():
        grad_copy(t).start()

    @pl.loop(1, 32)
    def _(i):
        grad_copy(lax.rem(t + i, 32)).start()

    load.wait()
    codes_scale = exp_ref[...]
    factor = jnp.where(
        codes_scale == -3, 0.125,
        jnp.where(codes_scale == -2, 0.25, jnp.where(codes_scale == -1, 0.5, jnp.where(codes_scale == 0, 1.0, 2.0))),
    ).astype(F32)
    lane = lax.broadcasted_iota(jnp.int32, (DIMS // BLKR, COLS), 1)
    spread = jnp.zeros((DIMS // BLKR, COLS), F32)
    for j in range(COLS // BLKC):
        spread = jnp.where(lax.div(lane, BLKC) == j, factor[:, j : j + 1], spread)
    GS[...] = spread

    arrived(px1)
    px2 = x_second(0, QR, QR + 48, CR)
    arrived(qz1)
    qz2 = z_ring_q(2)
    for rz in (1, 7):
        qx1[rz] = x_first(rz, 0, QR)

    @pl.loop(0, DIMS // BLKR)
    def _(b):
        rows = pl.ds(pl.multiple_of(b * BLKR, BLKR), BLKR)
        W[rows, :] = (W[rows, :].astype(F32) * GS[pl.ds(b, 1), :]).astype(BF16)

    wx = []
    for r in range(1, NX):
        block = y * NX + lax.rem(x + r, NX)
        rows = pl.ds(pl.multiple_of(block * ROWS + core * (ROWS // 2), 16), ROWS // 2)
        wx.append(start(copy(W.at[rows], WX.at[NX - r, y, core], dev_x(r))))

    arrived(px2)
    pz1 = z_ring_p(1)
    arrived(qx1[0])
    qx2[0] = x_second(0, 0, 48, QR)
    arrived(qz2)
    qz3 = z_ring_q(3)
    for rz in (2, 6):
        qx1[rz] = x_first(rz, 0, QR)

    def turn(lo, hi):
        @pl.loop(lo, hi)
        def _(b):
            WT[b, 0:COLS, :] = W[w_rows(b), :].astype(F32).T.astype(BF16)

    def y_unit(rel):
        return WX.at[1:NX, lax.rem(y + rel, NY), core]

    def y_ring(step):
        if step < 4:
            a = y_unit(NY - step + 1)
            right = copy(a, a, dev_y(1))
            b = y_unit(step - 1)
            left = copy(b, b, dev_y(NY - 1))
        else:
            a = WX.at[1:NX, lax.rem(y + 5, NY), core, 0:48]
            right = copy(a, a, dev_y(1))
            b = WX.at[1:NX, lax.rem(y + 3, NY), core, 48:80]
            left = copy(b, b, dev_y(NY - 1))
        return start(right), start(left)

    swaps = []

    def core_swap(rel):
        a = y_unit(rel)
        swaps.append(start(copy(a, a, other_core)))

    turn(0, 8)
    for c in wx:
        c.wait_recv()
    y1 = y_ring(1)
    core_swap(0)
    arrived(qz3)
    qz4 = z_ring_q(4)
    for rz in (3, 5):
        qx1[rz] = x_first(rz, 0, QR)
    for rz in (1, 7):
        arrived(qx1[rz])
        qx2[rz] = x_second(rz, 0, 48, QR)
    arrived(pz1)
    pz2 = z_ring_p(2)
    turn(8, 16)
    arrived(qz4)
    qx1[4] = x_first(4, 0, QR)
    for rz in (2, 6):
        arrived(qx1[rz])
        qx2[rz] = x_second(rz, 0, 48, QR)
    arrived(y1)
    y2 = y_ring(2)
    core_swap(1)
    core_swap(7)
    turn(16, 32)

    ACC[...] = jnp.zeros_like(ACC)

    def forward(rz):
        @pl.loop(0, NX)
        def _(rx):
            source = lax.rem(z + rz, NZ) * NX + lax.rem(x + rx, NX)
            slot = rz * NX + rx
            WT[source, COLS : COLS + RANK, :] = C[slot, ROWS:CR, 0:ROWS]
            ACC[...] += dot(WT[source], C[slot, 0:ROWS, :])

    arrived(qx2[0])
    forward(0)
    arrived(pz2)
    pz3 = z_ring_p(3)
    for rz in (3, 5):
        arrived(qx1[rz])
        qx2[rz] = x_second(rz, 0, 48, QR)
    arrived(y2)
    y3 = y_ring(3)
    core_swap(2)
    core_swap(6)
    for rz in (1, 7):
        arrived(qx2[rz])
        forward(rz)

    RT[...] = res_ref[...].astype(F32).T
    WX[0] = jnp.stack([W[w_rows(k * NX + x), :] for k in range(NZ)]).reshape(NZ, 2, ROWS // 2, COLS)
    grad_all = pltpu.make_async_copy(GR, GR, grecv_sem)
    grad_all.wait()
    residue = map_ref[...]
    block = lax.shift_right_logical(residue * 43691, 19)
    place = block * SLOT + (residue - block * OWNED)
    token = lax.broadcasted_iota(jnp.int32, (1, CROP), 1)
    place = jnp.where(token < len_ref[0], place, -1)
    chosen = (lax.broadcasted_iota(jnp.int32, (32 * SLOT, CROP), 0) == place).astype(F32).astype(BF16)
    upstream = dot(GR[...].reshape(32 * SLOT, COLS), chosen, ((0,), (0,)))
    gain = jnp.broadcast_to(gain_ref[...].astype(F32), (8, COLS)).T[:, 0:1]
    scaled = gain * upstream

    arrived(pz3)
    pz4 = z_ring_p(4)
    arrived(qx1[4])
    qx2[4] = x_second(4, 0, 48, QR)
    arrived(y3)
    y4 = y_ring(4)
    core_swap(3)
    core_swap(5)
    for rz in (2, 6):
        arrived(qx2[rz])
        forward(rz)
    for rz in (3, 5):
        arrived(qx2[rz])
        forward(rz)
    arrived(pz4)
    arrived(qx2[4])
    forward(4)

    inner = ACC[COLS : COLS + RANK, :].astype(BF16)
    hidden = ACC[0:COLS, :] + ADAPTER_SCALE * dot(up_ref[...], inner, ((0,), (0,))) + RT[...]
    ST[0:1, :] = jnp.sum(hidden, axis=0, keepdims=True)
    ST[1:2, :] = jnp.sum(hidden * hidden, axis=0, keepdims=True)
    ST[2:3, :] = jnp.sum(scaled, axis=0, keepdims=True)
    ST[3:4, :] = jnp.sum(scaled * hidden, axis=0, keepdims=True)
    ST[4:8, :] = jnp.zeros((4, CROP), F32)
    sx = [start(copy(ST, SX.at[r], dev_x(r))) for r in range(1, NX)]
    for c in sx:
        c.wait_recv()
    SZ[0] = (ST[...] + SX[1]) + (SX[2] + SX[3])
    sz = [start(copy(SZ.at[0], SZ.at[r], dev_z(r))) for r in range(1, NZ)]
    arrived(y4)
    core_swap(4)
    for c in sz:
        c.wait_recv()
    sums = jnp.sum(SZ[...], axis=0) / MODEL_WIDTH
    average = sums[0:1, :]
    variance = sums[1:2, :] - average * average
    inverse = lax.rsqrt(variance + 1e-05)
    first_mean = sums[2:3, :]
    second_mean = inverse * (sums[3:4, :] - average * first_mean)
    normed = (hidden - average) * inverse
    gradient = (inverse * (scaled - first_mean - normed * second_mean)).astype(BF16)
    for b in range(NBLOCK):
        HX[b, 0] = gradient[:, b * TOKEN_BLOCK : (b + 1) * TOKEN_BLOCK]

    def hx_first(b):
        return (
            start(copy(HX.at[b, 0], HX.at[b, 3], dev_x(1))),
            start(copy(HX.at[b, 0], HX.at[b, 1], dev_x(NX - 1))),
        )

    def hx_second(b):
        return (
            start(copy(HX.at[b, 3, 0:160], HX.at[b, 2, 0:160], dev_x(1))),
            start(copy(HX.at[b, 1, 160:COLS], HX.at[b, 2, 160:COLS], dev_x(NX - 1))),
        )

    h1 = [hx_first(b) for b in range(NBLOCK)]

    fh_ref[...] = (gain * normed).T.astype(BF16)
    hidden_gradient = gradient.astype(F32).T.astype(BF16)
    hg_ref[...] = hidden_gradient
    GA[:, 0:COLS] = ADAPTER_SCALE * dot(inner, hidden_gradient)
    for c in upc:
        c.wait_recv()
    for c in swaps:
        c.wait_recv()
    h2 = []
    for b in range(NBLOCK):
        arrived(h1[b])
        h2.append(hx_second(b))

    halves = NZ * ROWS // 2

    def partials(b):
        @pl.loop(0, 2)
        def _(h):
            total = jnp.zeros((halves, TOKEN_BLOCK), F32)
            for r in range(NX):
                w = WX[r, pl.ds(h * (NZ // 2), NZ // 2)].reshape(halves, COLS)
                total = total + dot(w, HX[b, r])
            PART[b, pl.ds(h * (NZ // 2), NZ // 2)] = total.reshape(NZ // 2, ROWS, TOKEN_BLOCK)

    def part(b, rel):
        return PART[b, lax.rem(z + rel, NZ)]

    HALF = ROWS // 2

    def rs_step(b, step):
        if step == 1:
            RS[b, 0, 0, 0:HALF] = part(b, 4)[0:HALF].astype(BF16)
            RS[b, 1, 0, 0:HALF] = part(b, 4)[HALF:ROWS].astype(BF16)
            right = copy(RS.at[b, 0, 0, 0:HALF], RR.at[b, 0, 0:HALF], dev_z(1))
            left = copy(RS.at[b, 1, 0, 0:HALF], LR.at[b, 0, 0:HALF], dev_z(NZ - 1))
        else:
            mine_right, mine_left = part(b, 5 - step), part(b, 3 + step)
            if step == 2:
                RS[b, 0, 1, 0:HALF] = (mine_right[0:HALF] + RR[b, 0, 0:HALF].astype(F32)).astype(BF16)
                RS[b, 0, 1, HALF:ROWS] = mine_right[HALF:ROWS].astype(BF16)
                RS[b, 1, 1, 0:HALF] = mine_left[0:HALF].astype(BF16)
                RS[b, 1, 1, HALF:ROWS] = (mine_left[HALF:ROWS] + LR[b, 0, 0:HALF].astype(F32)).astype(BF16)
            else:
                RS[b, 0, step - 1] = (mine_right + RR[b, step - 2].astype(F32)).astype(BF16)
                RS[b, 1, step - 1] = (mine_left + LR[b, step - 2].astype(F32)).astype(BF16)
            right = copy(RS.at[b, 0, step - 1], RR.at[b, step - 1], dev_z(1))
            left = copy(RS.at[b, 1, step - 1], LR.at[b, step - 1], dev_z(NZ - 1))
        return start(right), start(left)

    rs = {}
    for b in range(NBLOCK):
        arrived(h2[b])
        lanes = slice(b * TOKEN_BLOCK, (b + 1) * TOKEN_BLOCK)
        TZ[0, :, lanes] = jnp.zeros((RANK, TOKEN_BLOCK), F32)

        @pl.loop(0, NX)
        def _(r):
            TZ[0, :, lanes] += dot(UP4[r], HX[b, r])

        if b == NBLOCK - 1:
            tz = [start(copy(TZ.at[0], TZ.at[r], dev_z(r))) for r in range(1, NZ)]
        partials(b)
        rs[b, 1] = rs_step(b, 1)
        if b >= 1:
            arrived(rs[b - 1, 1])
            rs[b - 1, 2] = rs_step(b - 1, 2)
        if b >= 2:
            arrived(rs[b - 2, 2])
            rs[b - 2, 3] = rs_step(b - 2, 3)

    for c in tz:
        c.wait_recv()
    through_all = jnp.sum(TZ[...], axis=0).astype(BF16)
    GA[:, 384 : 384 + ROWS] = ADAPTER_SCALE * dot(through_all, ctx_ref[...])
    GA[:, 384 + ROWS :] = jnp.zeros((RANK, 96), F32)
    GA[:, COLS:384] = jnp.zeros((RANK, 64), F32)
    gc = start(copy(GA, GC, other_core))

    arrived(rs[2, 1])
    rs[2, 2] = rs_step(2, 2)
    arrived(rs[1, 2])
    rs[1, 3] = rs_step(1, 3)
    arrived(rs[0, 3])
    rs[0, 4] = rs_step(0, 4)
    gc.wait_recv()
    GY[0] = GA[...] + GC[...]
    gy = [start(copy(GY.at[0], GY.at[r], dev_y(r))) for r in range(1, NY)]
    arrived(rs[2, 2])
    rs[2, 3] = rs_step(2, 3)
    arrived(rs[1, 3])
    rs[1, 4] = rs_step(1, 4)
    arrived(rs[2, 3])
    rs[2, 4] = rs_step(2, 4)

    adapter = ADAPTER_SCALE * dot(down_ref[...], through_all)
    for b in range(NBLOCK):
        arrived(rs[b, 4])
        lanes = slice(b * TOKEN_BLOCK, (b + 1) * TOKEN_BLOCK)
        total = part(b, 0) + RR[b, 3].astype(F32) + LR[b, 3].astype(F32)
        cg_ref[:, lanes] = (total + adapter[:, lanes]).astype(BF16)

    for c in gy:
        c.wait_recv()
    grads = jnp.sum(GY[...], axis=0)
    ug_ref[...] = grads[:, 0:COLS]
    dg_ref[...] = grads[:, 384 : 384 + ROWS].T

    for c in pending:
        c.wait_send()

    @pl.when(self_target == 1)
    def _():
        pltpu.make_async_copy(GM.at[0:31], GM.at[0:31], gsend_sem).wait()

    @pl.when(self_target == 0)
    def _():
        pltpu.make_async_copy(GM, GM, gsend_sem).wait()


def on_device(grad, context, residual, gain, codes, exponents, down, up, residue_map, lengths):
    vmem = pl.BlockSpec(memory_space=pltpu.VMEM)
    return pl.pallas_call(
        kernel,
        out_shape=(
            jax.ShapeDtypeStruct((ROWS, CROP), BF16),
            jax.ShapeDtypeStruct((CROP, COLS), BF16),
            jax.ShapeDtypeStruct((ROWS, RANK), F32),
            jax.ShapeDtypeStruct((RANK, COLS), F32),
            jax.ShapeDtypeStruct((CROP, COLS), BF16),
        ),
        in_specs=[vmem] * 4
        + [pl.BlockSpec(memory_space=pl.ANY)]
        + [vmem] * 4
        + [pl.BlockSpec(memory_space=pltpu.SMEM)],
        out_specs=[vmem] * 5,
        scratch_shapes=[
            pltpu.VMEM((DIMS, COLS), BF16),
            pltpu.VMEM((NX * NZ, CR, CROP), BF16),
            pltpu.VMEM((NX * NZ, COLS + RANK, ROWS), BF16),
            pltpu.VMEM((NX, NZ, 2, ROWS // 2, COLS), BF16),
            pltpu.VMEM((32, SLOT, COLS), BF16),
            pltpu.VMEM((32, SLOT, COLS), BF16),
            pltpu.VMEM((COLS + RANK, CROP), F32),
            pltpu.VMEM((COLS, CROP), F32),
            pltpu.VMEM((NBLOCK, NX, COLS, TOKEN_BLOCK), BF16),
            pltpu.VMEM((NBLOCK, NZ, ROWS, TOKEN_BLOCK), F32),
            pltpu.VMEM((NBLOCK, 2, 4, ROWS, TOKEN_BLOCK), BF16),
            pltpu.VMEM((NBLOCK, 4, ROWS, TOKEN_BLOCK), BF16),
            pltpu.VMEM((NBLOCK, 4, ROWS, TOKEN_BLOCK), BF16),
            pltpu.VMEM((NX, RANK, COLS), BF16),
            pltpu.VMEM((8, CROP), F32),
            pltpu.VMEM((NX, 8, CROP), F32),
            pltpu.VMEM((NZ, 8, CROP), F32),
            pltpu.VMEM((8, 128), F32),
            pltpu.VMEM((NZ, RANK, CROP), F32),
            pltpu.VMEM((RANK, 640), F32),
            pltpu.VMEM((RANK, 640), F32),
            pltpu.VMEM((NY, RANK, 640), F32),
            pltpu.VMEM((DIMS // BLKR, COLS), F32),
            pltpu.SemaphoreType.DMA((SENDS,)),
            pltpu.SemaphoreType.DMA((SENDS,)),
            pltpu.SemaphoreType.DMA,
            pltpu.SemaphoreType.DMA,
            pltpu.SemaphoreType.DMA,
        ],
        compiler_params=pltpu.CompilerParams(
            collective_id=0, has_side_effects=True, vmem_limit_bytes=56 * 1024 * 1024
        ),
        cost_estimate=pl.CostEstimate(flops=2 * 2 * CROP * DIMS * COLS, bytes_accessed=8 << 20, transcendentals=0),
    )(grad, context, residual, gain.reshape(1, COLS), codes, exponents, down, up, residue_map, lengths)


def solution(mesh):
    in_specs = (
        P(("dp", "tensor", "section"), None),
        P(("dp", "section"), "tensor"),
        P(("dp", "section"), "tensor"),
        P("tensor"),
        P(None, "tensor"),
        P(None, "tensor"),
        P("tensor", None),
        P(None, "tensor"),
        P(("dp", "section"), None),
        P(("dp", "section")),
    )
    out_specs = (
        P("tensor", ("dp", "section")),
        P(("dp", "section"), "tensor"),
        P("tensor", None),
        P(None, "tensor"),
        P(("dp", "section"), "tensor"),
    )
    return jax.shard_map(
        on_device, mesh=mesh, in_specs=in_specs, out_specs=out_specs, check_vma=False
    )
```

time: 583 us -> 135 us (0.23)
  the two profiles are of different devices: /device:TPU:6 before, /device:TPU:1 now
where the time goes in v1:
time: 135 us; the launch traced here: 134 us
  Pallas kernels  111 us (82%)
  local copies, waits for them, and re-layouts  21.5 us (16%)
    pallas_call x1, Pallas kernels, on_device(): pl.pallas_call(kernel, out_shape=(jax.ShapeDtypeStruct((ROWS, CROP), BF16...  111 us
    unnamed x7, local copies, waits for them, and re-layouts  15.1 us
    pallas_call x3, local copies, waits for them, and re-layouts, on_device(): pl.pallas_call(kernel, out_shape=(jax.ShapeDtypeStruct((ROWS, CROP), BF16...  5.18 us

profile of v1, /device:TPU:1, one launch (start us, length us, event | category | flops | bytes accessed | tf_op | source)
XLA Modules:
  0.0 134.2 jit_solution(3227023111931922137)
XLA Ops:
  1.3 1.2 reshape.13.gain_ref
  2.5 1.4 %copy.18.exp_ref = s32[40,5]{1,0:T(8,128)} copy(s32[40,5]{0,1:T(8,128)} %param.15) | data formatting | bytes 1600 | tf_op args[5]
  3.9 1.4 %copy.19.down_ref = bf16[160,16]{1,0:T(8,128)(2,1)} copy(bf16[160,16]{0,1:T(8,128)(2,1)} %param.16) | data formatting | bytes 10240 | tf_op args[6]
  5.3 1.7 %copy.15.ctx_ref = bf16[384,160]{1,0:T(8,128)(2,1)} copy(bf16[384,160]{0,1:T(8,128)(2,1)} %param.11) | data formatting | bytes 245760 | tf_op args[1]
  7.0 1.8 %copy.16.res_ref = bf16[384,320]{1,0:T(8,128)(2,1)} copy(bf16[384,320]{0,1:T(8,128)(2,1)} %param.12) | data formatting | bytes 491520 | tf_op args[2]
  8.9 5.8 %copy.17.codes_ref = bf16[5120,320]{1,0:T(8,128)(2,1)} copy(bf16[5120,320]{0,1:T(8,128)(2,1)} %param.14) | data formatting | bytes 6553600 | tf_op args[4]
  14.7 111.5 %shard_map.137 = (bf16[160,384]{1,0:T(8,128)(2,1)}, bf16[384,320]{1,0:T(8,128)(2,1)}, f32[160,16]{1,0:T(8,128)}, f32[16,320]{1,0:T(8,128)}, bf16[384,320]{1,0:T(8,128)(2,1)}) custom-call(bf16[12,10240]{1,0:T(8,128)(2,1)} %grad_ref.1, bf16[384,160]{1,0:T(8,128)(2,1)} %copy.15.ctx_ref, bf16[384,320]{1,0:T(8,128)(2,1)} %copy.16.res_ref, ...), custom_call_target="tpu_custom_call" | custom-call | flops 2516582400 | bytes 8388608 | tf_op jit(solution)/shard_map/pallas_call | solution.py:502
  126.2 1.6 %copy.21 = f32[160,16]{0,1:T(8,128)} copy(f32[160,16]{1,0:T(8,128)} %get-tuple-element.7) | data formatting | bytes 20480 | tf_op jit(solution)/shard_map/pallas_call | solution.py:502
  127.7 1.8 %copy.20 = bf16[384,320]{0,1:T(8,128)(2,1)} copy(bf16[384,320]{1,0:T(8,128)(2,1)} %get-tuple-element.6) | data formatting | bytes 491520 | tf_op jit(solution)/shard_map/pallas_call | solution.py:502
  129.5 1.8 %copy.22 = bf16[384,320]{0,1:T(8,128)(2,1)} copy(bf16[384,320]{1,0:T(8,128)(2,1)} %get-tuple-element.9) | data formatting | bytes 491520 | tf_op jit(solution)/shard_map/pallas_call | solution.py:502
  131.3 1.6 %copy.26 = bf16[160,384]{1,0:T(8,128)(2,1)} copy(bf16[160,384]{1,0:T(8,128)(2,1)} %get-tuple-element.15) | data formatting | bytes 245760
  132.9 1.3 %copy.27 = f32[16,320]{1,0:T(8,128)} copy(f32[16,320]{1,0:T(8,128)} %get-tuple-element.18) | data formatting | bytes 40960

commit v2 on v1

v2 whole, which is shorter than its diff:
```python
import functools

import jax
import jax.numpy as jnp
from jax import lax
from jax.experimental import pallas as pl
from jax.experimental.pallas import tpu as pltpu
from jax.sharding import PartitionSpec as P

MODEL_WIDTH = 10240
DIMS = 5120
ADAPTER_SCALE = 2.0
CROP = 384
COLS = 320
ROWS = 160
RANK = 16
NX = 4
NZ = 8
NY = 8
BLKR = 128
BLKC = 64
OWNED = 12
SLOT = 16
F32 = jnp.float32
BF16 = jnp.bfloat16
MESH = pl.DeviceIdType.MESH
QR = 112
PH = 32
TOKEN_BLOCK = 128
NBLOCK = CROP // TOKEN_BLOCK

SENDS = 200


def dot(a, b, dims=((1,), (0,))):
    return lax.dot_general(a, b, (dims, ((), ())), preferred_element_type=F32)


def kernel(
    grad_hbm, ctx_hbm, res_hbm, gain_ref, codes_hbm, exp_hbm, down_hbm, up_hbm, map_hbm, len_ref,
    cg_out, hg_out, dg_out, ug_out, fh_out,
    W, C, DX, DN, SLAB, WS, WT, WX, GI, GM, A1, A2, A3, ACC, HX, PART, RS, RR, LR, ST, SX, SZ, TX, TZ,
    UA, UC, UY, DA, DC, DY, GS, RES, EXP, DIN, UP, MAP, CG, HG, DG, UG, FH,
    send_sem, recv_sem, load_sem,
):
    dp = lax.axis_index("dp")
    t = lax.axis_index("tensor")
    sec = lax.axis_index("section")
    x = lax.rem(t, NX)
    z = lax.div(t, NX)
    core = lax.rem(dp, 2)
    y = sec * (NY // 2) + lax.div(dp, 2)

    def dev_x(r):
        return (dp, z * NX + lax.rem(x + r, NX), sec)

    def dev_z(r):
        return (dp, lax.rem(z + r, NZ) * NX + x, sec)

    def dev_y(r):
        other = lax.rem(y + r, NY)
        return (lax.rem(other, NY // 2) * 2 + core, t, lax.div(other, NY // 2))

    other_core = (dp + 1 - 2 * core, t, sec)
    before, after, opposite = lax.rem(x + 3, NX), lax.rem(x + 1, NX), lax.rem(x + 2, NX)

    group = NX * ROWS

    def w_lanes(index):
        return pl.ds(pl.multiple_of(index * group, 128), group)

    local_copies = [0]

    def local_copy(src, dst):
        k = local_copies[0]
        local_copies[0] += 1
        c = pltpu.make_async_copy(src, dst, load_sem.at[k])
        c.start()
        return c

    load_ctx = local_copy(ctx_hbm, C.at[x])
    load_grad = local_copy(grad_hbm, GI)
    load_down = local_copy(down_hbm, DIN)
    load_exp = local_copy(exp_hbm, EXP)
    load_codes = local_copy(codes_hbm, W.at[0:COLS])
    load_rest = [local_copy(map_hbm, MAP), local_copy(up_hbm, UP), local_copy(res_hbm, RES)]

    barrier = pltpu.get_barrier_semaphore()

    def greet(device):
        pl.semaphore_signal(barrier, inc=1, device_id=device, device_id_type=MESH)

    for r in range(1, NX):
        greet(dev_x(r))
    for r in range(1, NZ):
        greet(dev_z(r))
    for r in range(1, NY):
        greet(dev_y(r))
    greet(other_core)

    counter = [0]

    def copy(src, dst, device):
        k = counter[0]
        counter[0] += 1
        return pltpu.make_async_remote_copy(
            src_ref=src, dst_ref=dst, send_sem=send_sem.at[k], recv_sem=recv_sem.at[k],
            device_id=device, device_id_type=MESH,
        )

    pending = []

    def start(c):
        c.start()
        pending.append(c)
        return c

    def arrived(pair):
        for c in pair:
            c.wait_recv()

    load_down.wait()
    DX[x] = jnp.concatenate([DIN[...], jnp.zeros((RANK, 96), BF16)], axis=1)
    load_ctx.wait()

    pl.semaphore_wait(barrier, (NX - 1) + (NZ - 1) + (NY - 1) + 1)

    def z_ring(step, column, lo, mid, hi):
        if step < 4:
            right = copy(
                C.at[((NZ - step + 1) % NZ) * NX + column, lo:hi], C.at[(NZ - step) * NX + column, lo:hi], dev_z(1)
            )
            left = copy(C.at[(step - 1) * NX + column, lo:hi], C.at[step * NX + column, lo:hi], dev_z(NZ - 1))
        else:
            right = copy(C.at[5 * NX + column, lo:mid], C.at[4 * NX + column, lo:mid], dev_z(1))
            left = copy(C.at[3 * NX + column, mid:hi], C.at[4 * NX + column, mid:hi], dev_z(NZ - 1))
        return start(right), start(left)

    def qz(step):
        return z_ring(step, x, 0, 64, QR)

    def pz(step, column):
        return z_ring(step, column, QR, QR + PH, ROWS)

    def x_first(rz, lo, hi):
        own = C.at[rz * NX + x, lo:hi]
        return start(copy(own, own, dev_x(1))), start(copy(own, own, dev_x(NX - 1)))

    def x_second(rz, lo, mid, hi):
        a = C.at[rz * NX + before, lo:mid]
        b = C.at[rz * NX + after, mid:hi]
        return start(copy(a, a, dev_x(1))), start(copy(b, b, dev_x(NX - 1)))

    qz_c, qx1, qx2, pz_c = {}, {}, {}, {}

    def q_first(*places):
        for rz in places:
            qx1[rz] = x_first(rz, 0, QR)

    def q_second(*places):
        for rz in places:
            arrived(qx1[rz])
            qx2[rz] = x_second(rz, 0, 64 if rz % 2 == 0 else 48, QR)

    def p_next(step, column, name):
        if step > 1:
            arrived(pz_c[name, step - 1])
        pz_c[name, step] = pz(step, column)

    def dn_ring(step):
        if step < 4:
            right = copy(DN.at[(NZ - step + 1) % NZ], DN.at[NZ - step], dev_z(1))
            left = copy(DN.at[step - 1], DN.at[step], dev_z(NZ - 1))
            return start(right), start(left)
        return (start(copy(DN.at[5], DN.at[4], dev_z(1))),)

    qz_c[1] = qz(1)
    px1 = x_first(0, QR, ROWS)
    dx = [start(copy(DX.at[x], DX.at[x], dev_x(r))) for r in range(1, NX)]
    p_next(1, x, "own")
    q_first(0)

    load_exp.wait()
    codes_scale = EXP[...]
    factor = jnp.where(
        codes_scale == -3, 0.125,
        jnp.where(codes_scale == -2, 0.25, jnp.where(codes_scale == -1, 0.5, jnp.where(codes_scale == 0, 1.0, 2.0))),
    ).astype(F32)
    for j in range(COLS // BLKC):
        GS[j * BLKC : (j + 1) * BLKC, :] = jnp.broadcast_to(factor[j : j + 1, :], (BLKC, DIMS // BLKR))
    load_codes.wait()

    picked = (
        lax.broadcasted_iota(jnp.int32, (DIMS // BLKR, 128), 0)
        == y * (group // BLKR) + lax.broadcasted_iota(jnp.int32, (DIMS // BLKR, 128), 1)
    )
    slab_scale = dot(GS[...].astype(BF16), picked.astype(F32).astype(BF16))
    for i in range(group // BLKR):
        lanes = pl.ds(pl.multiple_of(y * group + i * BLKR, BLKR), BLKR)
        SLAB[:, i * BLKR : (i + 1) * BLKR] = (W[0:COLS, lanes].astype(F32) * slab_scale[:, i : i + 1]).astype(BF16)
    WS[...] = SLAB[...].T.reshape(NX, 2, ROWS // 2, COLS)
    wx = []
    for r in range(1, NX):
        wx.append(start(copy(WS.at[lax.rem(x + r, NX), core], WX.at[NX - r, y, core], dev_x(r))))

    arrived(qz_c[1])
    qz_c[2] = qz(2)
    q_first(1, 7)
    arrived(px1)
    px2 = x_second(0, QR, QR + PH, ROWS)
    p_next(1, before, "before")
    p_next(1, after, "after")
    p_next(2, x, "own")
    def y_unit(rel):
        return WX.at[1:NX, lax.rem(y + rel, NY), core]

    def y_ring(step):
        if step < 4:
            a = y_unit(NY - step + 1)
            b = y_unit(step - 1)
        else:
            a = WX.at[1:NX, lax.rem(y + 5, NY), core, 0:48]
            b = WX.at[1:NX, lax.rem(y + 3, NY), core, 48:80]
        return start(copy(a, a, dev_y(1))), start(copy(b, b, dev_y(NY - 1)))

    swaps = []

    def core_swap(*places):
        for rel in places:
            a = y_unit(rel)
            swaps.append(start(copy(a, a, other_core)))

    for c in wx:
        c.wait_recv()
    y1 = y_ring(1)
    core_swap(0)
    for c in dx:
        c.wait_recv()
    DN[0] = jnp.concatenate([DX[i, :, 0:ROWS] for i in range(NX)], axis=1)
    dn1 = dn_ring(1)

    load_grad.wait()
    for i in range(32):
        g = GI[:, i * COLS : (i + 1) * COLS].astype(F32)
        last = [g[4 * q : 4 * q + 4, 256:COLS] for q in range(3)]
        side = jnp.concatenate(last + [jnp.zeros((4, 64), F32)], axis=1)
        GM[i % NX, i // NX] = jnp.concatenate([g[:, 0:256], side], axis=0).astype(BF16)
    gx = [start(copy(GM.at[lax.rem(x + r, NX)], A1.at[x], dev_x(r))) for r in range(1, NX)]
    A1[x] = GM[x]

    for b in range(DIMS // BLKR):
        lanes = slice(b * BLKR, (b + 1) * BLKR)
        W[0:COLS, lanes] = (W[0:COLS, lanes].astype(F32) * GS[:, b : b + 1]).astype(BF16)

    q_second(0)
    arrived(qz_c[2])
    qz_c[3] = qz(3)
    q_first(2, 6)
    arrived(px2)
    p_next(1, opposite, "opposite")

    for c in gx:
        c.wait_recv()
    A2[z] = A1[:, z]
    gz = [start(copy(A1.at[:, lax.rem(z + r, NZ)], A2.at[z], dev_z(r))) for r in range(1, NZ)]

    q_second(1, 7)
    p_next(2, before, "before")
    p_next(2, after, "after")
    p_next(3, x, "own")
    arrived(dn1)
    dn2 = dn_ring(2)

    def turn(k):
        WT[...] = W[0:COLS, pl.ds(pl.multiple_of(k * group + x * BLKR, BLKR), 256)].T
        rows = WT[pl.ds(pl.multiple_of(x * 32, 32), ROWS), :]
        WX[0, k] = rows.reshape(2, ROWS // 2, COLS)


    arrived(qz_c[3])
    qz_c[4] = qz(4)
    q_first(3, 5)
    p_next(2, opposite, "opposite")
    q_second(2, 6)
    p_next(3, before, "before")
    p_next(3, after, "after")
    p_next(4, x, "own")
    arrived(dn2)
    dn3 = dn_ring(3)
    for k in range(NZ // 2):
        turn(k)
    arrived(y1)
    y2 = y_ring(2)
    core_swap(1, 7)

    arrived(qz_c[4])
    q_first(4)
    p_next(3, opposite, "opposite")
    q_second(3, 5)
    p_next(4, before, "before")
    p_next(4, after, "after")
    arrived(dn3)
    dn4 = dn_ring(4)
    for c in gz:
        c.wait_recv()
    ga = start(copy(A2.at[pl.ds((1 - sec) * (NZ // 2), NZ // 2)], A3, (dp, t, 1 - sec)))
    for k in range(NZ // 2, NZ):
        turn(k)

    ACC[...] = jnp.zeros_like(ACC)

    def forward(rz):
        if rz == 4:
            for name in ("own", "before", "after", "opposite"):
                arrived(pz_c[name, 4])
        arrived(qx2[rz])
        lanes = w_lanes(lax.rem(z + rz, NZ))
        W[COLS : COLS + RANK, lanes] = DN[rz]
        ACC[...] += dot(W[:, lanes], C[rz * NX : (rz + 1) * NX].reshape(group, CROP))

    q_second(4)
    p_next(4, opposite, "opposite")
    forward(0)
    arrived(y2)
    y3 = y_ring(3)
    core_swap(2, 6)
    forward(1)
    forward(7)

    for c in load_rest:
        c.wait()
    ga.wait_recv()
    residue = MAP[...]
    block = lax.shift_right_logical(residue * 43691, 19)
    row = residue - block * OWNED
    quarter = lax.shift_right_logical(row, 2)
    token = lax.broadcasted_iota(jnp.int32, (1, CROP), 1)
    valid = token < len_ref[0]
    parity = block & 1
    slot = lax.shift_right_logical(block, 1) + jnp.where(parity == sec, 0, 16)
    place = jnp.where(valid, slot * SLOT + row, -1)
    place_last = jnp.where(valid, slot * SLOT + OWNED + (row - quarter * 4), -1)
    index = lax.broadcasted_iota(jnp.int32, (32 * SLOT, CROP), 0)
    mine = A2[pl.ds(sec * (NZ // 2), NZ // 2)].reshape(16 * SLOT, 256)
    rows = jnp.concatenate([mine, A3[...].reshape(16 * SLOT, 256)], axis=0)
    most = dot(rows, (index == place).astype(F32).astype(BF16), ((0,), (0,)))
    last = dot(rows, (index == place_last).astype(F32).astype(BF16), ((0,), (0,)))
    last = jnp.where(quarter == 0, last[0:64], jnp.where(quarter == 1, last[64:128], last[128:192]))
    upstream = jnp.concatenate([most, last], axis=0)
    gain = jnp.broadcast_to(gain_ref[...].astype(F32).reshape(1, COLS), (8, COLS)).T[:, 0:1]
    scaled = gain * upstream

    forward(2)
    forward(6)
    forward(3)
    forward(5)
    arrived(y3)
    y4 = y_ring(4)
    core_swap(3, 5)
    arrived(dn4)
    forward(4)

    inner = ACC[COLS : COLS + RANK, :].astype(BF16)
    hidden = ACC[0:COLS, :] + ADAPTER_SCALE * dot(UP[...], inner, ((0,), (0,))) + RES[...].astype(F32)
    ST[0:1, :] = jnp.sum(hidden, axis=0, keepdims=True)
    ST[1:2, :] = jnp.sum(hidden * hidden, axis=0, keepdims=True)
    ST[2:3, :] = jnp.sum(scaled, axis=0, keepdims=True)
    ST[3:4, :] = jnp.sum(scaled * hidden, axis=0, keepdims=True)
    sx = [start(copy(ST, SX.at[r], dev_x(r))) for r in range(1, NX)]
    for c in sx:
        c.wait_recv()
    SZ[0] = (ST[...] + SX[1]) + (SX[2] + SX[3])
    sz = [start(copy(SZ.at[0], SZ.at[r], dev_z(r))) for r in range(1, NZ)]
    arrived(y4)
    core_swap(4)
    for c in sz:
        c.wait_recv()
    sums = jnp.sum(SZ[...], axis=0) / MODEL_WIDTH
    average = sums[0:1, :]
    variance = sums[1:2, :] - average * average
    inverse = lax.rsqrt(variance + 1e-05)
    first_mean = sums[2:3, :]
    second_mean = inverse * (sums[3:4, :] - average * first_mean)
    normed = (hidden - average) * inverse
    gradient = (inverse * (scaled - first_mean - normed * second_mean)).astype(BF16)
    for b in range(NBLOCK):
        HX[b, 0] = gradient[:, b * TOKEN_BLOCK : (b + 1) * TOKEN_BLOCK]

    def hx_first(b):
        return (
            start(copy(HX.at[b, 0], HX.at[b, 3], dev_x(1))),
            start(copy(HX.at[b, 0], HX.at[b, 1], dev_x(NX - 1))),
        )

    def hx_second(b):
        arrived(h1[b])
        return (
            start(copy(HX.at[b, 3, 0:160], HX.at[b, 2, 0:160], dev_x(1))),
            start(copy(HX.at[b, 1, 160:COLS], HX.at[b, 2, 160:COLS], dev_x(NX - 1))),
        )

    h1 = [hx_first(0)]
    TX[0] = dot(UP[...], gradient)
    tx = [start(copy(TX.at[0], TX.at[r], dev_x(r))) for r in range(1, NX)]
    h1 += [hx_first(1), hx_first(2)]
    HG[...] = gradient
    out_hg = local_copy(HG, hg_out)
    FH[...] = (gain * normed).astype(BF16)
    out_fh = local_copy(FH, fh_out)
    UA[...] = ADAPTER_SCALE * dot(inner, gradient, ((1,), (1,)))
    uc = start(copy(UA, UC, other_core))
    for c in tx:
        c.wait_recv()
    TZ[0] = (TX[0] + TX[1]) + (TX[2] + TX[3])
    tz = [start(copy(TZ.at[0], TZ.at[r], dev_z(r))) for r in range(1, NZ)]
    h2 = [hx_second(0)]
    uc.wait_recv()
    UY[0] = UA[...] + UC[...]
    uy = [start(copy(UY.at[0], UY.at[r], dev_y(r))) for r in range(1, NY)]
    for c in swaps:
        c.wait_recv()
    h2.append(hx_second(1))

    halves = NZ * ROWS // 2

    def partials(b):
        arrived(h2[b])

        @pl.loop(0, 2)
        def _(h):
            total = jnp.zeros((halves, TOKEN_BLOCK), F32)
            for r in range(NX):
                w = WX[r, pl.ds(h * (NZ // 2), NZ // 2)].reshape(halves, COLS)
                total = total + dot(w, HX[b, r])
            PART[b, pl.ds(h * (NZ // 2), NZ // 2)] = total.reshape(NZ // 2, ROWS, TOKEN_BLOCK)

    def part(b, rel):
        return PART[b, lax.rem(z + rel, NZ)]

    HALF = ROWS // 2
    rs = {}

    def rs_step(b, step):
        if step == 1:
            RS[b, 0, 0, 0:HALF] = part(b, 4)[0:HALF].astype(BF16)
            RS[b, 1, 0, 0:HALF] = part(b, 4)[HALF:ROWS].astype(BF16)
            right = copy(RS.at[b, 0, 0, 0:HALF], RR.at[b, 0, 0:HALF], dev_z(1))
            left = copy(RS.at[b, 1, 0, 0:HALF], LR.at[b, 0, 0:HALF], dev_z(NZ - 1))
        else:
            arrived(rs[b, step - 1])
            mine_right, mine_left = part(b, 5 - step), part(b, 3 + step)
            if step == 2:
                RS[b, 0, 1, 0:HALF] = (mine_right[0:HALF] + RR[b, 0, 0:HALF].astype(F32)).astype(BF16)
                RS[b, 0, 1, HALF:ROWS] = mine_right[HALF:ROWS].astype(BF16)
                RS[b, 1, 1, 0:HALF] = mine_left[0:HALF].astype(BF16)
                RS[b, 1, 1, HALF:ROWS] = (mine_left[HALF:ROWS] + LR[b, 0, 0:HALF].astype(F32)).astype(BF16)
            else:
                RS[b, 0, step - 1] = (mine_right + RR[b, step - 2].astype(F32)).astype(BF16)
                RS[b, 1, step - 1] = (mine_left + LR[b, step - 2].astype(F32)).astype(BF16)
            right = copy(RS.at[b, 0, step - 1], RR.at[b, step - 1], dev_z(1))
            left = copy(RS.at[b, 1, step - 1], LR.at[b, step - 1], dev_z(NZ - 1))
        rs[b, step] = (start(right), start(left))

    partials(0)
    rs_step(0, 1)
    h2.append(hx_second(2))
    for c in tz:
        c.wait_recv()
    through_all = jnp.sum(TZ[...], axis=0).astype(BF16)
    DA[...] = ADAPTER_SCALE * dot(through_all, C[x], ((1,), (1,)))
    dc = start(copy(DA, DC, other_core))
    adapter = ADAPTER_SCALE * dot(DIN[...], through_all, ((0,), (0,)))
    rs_step(0, 2)
    partials(1)
    rs_step(1, 1)
    dc.wait_recv()
    DY[0] = DA[...] + DC[...]
    dy = [start(copy(DY.at[0], DY.at[r], dev_y(r))) for r in range(1, NY)]
    rs_step(0, 3)
    rs_step(1, 2)
    partials(2)
    rs_step(2, 1)
    rs_step(0, 4)
    rs_step(1, 3)
    rs_step(2, 2)
    rs_step(1, 4)
    for c in uy:
        c.wait_recv()
    UG[...] = jnp.sum(UY[...], axis=0)
    out_ug = local_copy(UG, ug_out)
    rs_step(2, 3)
    for c in dy:
        c.wait_recv()
    DG[...] = jnp.sum(DY[...], axis=0)
    out_dg = local_copy(DG, dg_out)
    rs_step(2, 4)
    for b in range(NBLOCK):
        arrived(rs[b, 4])
        lanes = slice(b * TOKEN_BLOCK, (b + 1) * TOKEN_BLOCK)
        total = part(b, 0) + RR[b, 3].astype(F32) + LR[b, 3].astype(F32)
        CG[:, lanes] = (total + adapter[:, lanes]).astype(BF16)
    out_cg = local_copy(CG, cg_out)

    for c in pending:
        c.wait_send()

    for c in (out_hg, out_fh, out_ug, out_dg, out_cg):
        c.wait()


def finish(*refs):
    for array, out in zip(refs[:5], refs[5:]):
        out[...] = array[...]


def on_device(grad, context, residual, gain, codes, exponents, down, up, residue_map, lengths):
    vmem = pl.BlockSpec(memory_space=pltpu.VMEM)
    anywhere = pl.BlockSpec(memory_space=pl.ANY)
    shapes = (
        jax.ShapeDtypeStruct((ROWS, CROP), BF16),
        jax.ShapeDtypeStruct((COLS, CROP), BF16),
        jax.ShapeDtypeStruct((RANK, ROWS), F32),
        jax.ShapeDtypeStruct((RANK, COLS), F32),
        jax.ShapeDtypeStruct((COLS, CROP), BF16),
    )
    results = pl.pallas_call(
        kernel,
        out_shape=shapes,
        in_specs=[anywhere] * 3 + [vmem] + [anywhere] * 5 + [pl.BlockSpec(memory_space=pltpu.SMEM)],
        out_specs=[anywhere] * 5,
        scratch_shapes=[
            pltpu.VMEM((COLS + RANK, DIMS), BF16),
            pltpu.VMEM((NX * NZ, ROWS, CROP), BF16),
            pltpu.VMEM((NX, RANK, 256), BF16),
            pltpu.VMEM((NZ, RANK, NX * ROWS), BF16),
            pltpu.VMEM((COLS, NX * ROWS), BF16),
            pltpu.VMEM((NX, 2, ROWS // 2, COLS), BF16),
            pltpu.VMEM((256, COLS), BF16),
            pltpu.VMEM((NX, NZ, 2, ROWS // 2, COLS), BF16),
            pltpu.VMEM((OWNED, MODEL_WIDTH), BF16),
            pltpu.VMEM((NX, NZ, SLOT, 256), BF16),
            pltpu.VMEM((NX, NZ, SLOT, 256), BF16),
            pltpu.VMEM((NZ, NX, SLOT, 256), BF16),
            pltpu.VMEM((NZ // 2, NX, SLOT, 256), BF16),
            pltpu.VMEM((COLS + RANK, CROP), F32),
            pltpu.VMEM((NBLOCK, NX, COLS, TOKEN_BLOCK), BF16),
            pltpu.VMEM((NBLOCK, NZ, ROWS, TOKEN_BLOCK), F32),
            pltpu.VMEM((NBLOCK, 2, 4, ROWS, TOKEN_BLOCK), BF16),
            pltpu.VMEM((NBLOCK, 4, ROWS, TOKEN_BLOCK), BF16),
            pltpu.VMEM((NBLOCK, 4, ROWS, TOKEN_BLOCK), BF16),
            pltpu.VMEM((4, CROP), F32),
            pltpu.VMEM((NX, 4, CROP), F32),
            pltpu.VMEM((NZ, 4, CROP), F32),
            pltpu.VMEM((NX, RANK, CROP), F32),
            pltpu.VMEM((NZ, RANK, CROP), F32),
            pltpu.VMEM((RANK, COLS), F32),
            pltpu.VMEM((RANK, COLS), F32),
            pltpu.VMEM((NY, RANK, COLS), F32),
            pltpu.VMEM((RANK, ROWS), F32),
            pltpu.VMEM((RANK, ROWS), F32),
            pltpu.VMEM((NY, RANK, ROWS), F32),
            pltpu.VMEM((COLS, DIMS // BLKR), F32),
            pltpu.VMEM((COLS, CROP), BF16),
            pltpu.VMEM((COLS // BLKC, DIMS // BLKR), jnp.int32),
            pltpu.VMEM((RANK, ROWS), BF16),
            pltpu.VMEM((RANK, COLS), BF16),
            pltpu.VMEM((1, CROP), jnp.int32),
            pltpu.VMEM((ROWS, CROP), BF16),
            pltpu.VMEM((COLS, CROP), BF16),
            pltpu.VMEM((RANK, ROWS), F32),
            pltpu.VMEM((RANK, COLS), F32),
            pltpu.VMEM((COLS, CROP), BF16),
            pltpu.SemaphoreType.DMA((SENDS,)),
            pltpu.SemaphoreType.DMA((SENDS,)),
            pltpu.SemaphoreType.DMA((16,)),
        ],
        compiler_params=pltpu.CompilerParams(
            collective_id=0, has_side_effects=True, vmem_limit_bytes=56 * 1024 * 1024
        ),
        cost_estimate=pl.CostEstimate(flops=2 * 2 * CROP * DIMS * COLS, bytes_accessed=8 << 20, transcendentals=0),
    )(grad, context.T, residual.T, gain, codes.T, exponents.T, down.T, up, residue_map, lengths)
    cg, hg, dg, ug, fh = pl.pallas_call(
        finish,
        out_shape=shapes,
        in_specs=[vmem] * 5,
        out_specs=[vmem] * 5,
    )(*results)
    return cg, hg.T, dg.T, ug, fh.T


def solution(mesh):
    in_specs = (
        P(("dp", "tensor", "section"), None),
        P(("dp", "section"), "tensor"),
        P(("dp", "section"), "tensor"),
        P("tensor"),
        P(None, "tensor"),
        P(None, "tensor"),
        P("tensor", None),
        P(None, "tensor"),
        P(("dp", "section"), None),
        P(("dp", "section")),
    )
    out_specs = (
        P("tensor", ("dp", "section")),
        P(("dp", "section"), "tensor"),
        P("tensor", None),
        P(None, "tensor"),
        P(("dp", "section"), "tensor"),
    )
    return jax.shard_map(
        on_device, mesh=mesh, in_specs=in_specs, out_specs=out_specs, check_vma=False
    )
```

time: 135 us -> 108 us (0.80)
  the two profiles are of different devices: /device:TPU:1 before, /device:TPU:6 now
where the time goes in v2:
time: 108 us; the launch traced here: 107 us
  Pallas kernels  106 us (98%)
  between operations  1.29 us (1%)
    pallas_call x1, Pallas kernels, on_device(): pl.pallas_call(kernel, out_shape=shapes, in_specs=[anywhere] * 3 + [vmem]...  104 us

profile of v2, /device:TPU:6, one launch (start us, length us, event | category | flops | bytes accessed | tf_op | source)
XLA Modules:
  0.0 107.3 jit_solution(11736405036700803834)
XLA Ops:
  1.3 104.0 %shard_map.137 = (bf16[160,384]{1,0:T(8,128)(2,1)}, bf16[320,384]{1,0:T(8,128)(2,1)}, f32[16,160]{1,0:T(8,128)}, f32[16,320]{1,0:T(8,128)}, bf16[320,384]{1,0:T(8,128)(2,1)}) custom-call(bf16[12,10240]{1,0:T(8,128)(2,1)} %grad_hbm.1, bf16[160,384]{1,0:T(8,128)(2,1)} %bitcast.12, bf16[320,384]{1,0:T(8,128)(2,1)} %bitcast.9, bf16[320]{0:T(512)(128)(2,1)} %gain_ref.1, ...), custom_call_target="tpu_custom_call" | custom-call | flops 2516582400 | bytes 8388608 | tf_op jit(solution)/shard_map/pallas_call | solution.py:526
  105.3 2.0 %shard_map.138 = (bf16[160,384]{1,0:T(8,128)(2,1)}, bf16[320,384]{1,0:T(8,128)(2,1)}, f32[16,160]{1,0:T(8,128)}, f32[16,320]{1,0:T(8,128)}, bf16[320,384]{1,0:T(8,128)(2,1)}) custom-call(bf16[160,384]{1,0:T(8,128)(2,1)} %get-tuple-element.15.refs_0_, bf16[320,384]{1,0:T(8,128)(2,1)} %get-tuple-element.16.refs_1_, f32[16,160]{1,0:T(8,128)} %get-tuple-element.17.refs_2_, ...), custom_call_target="tpu_custom_call" | custom-call | tf_op jit(solution)/shard_map/pallas_call | solution.py:582

commit v3 on v2

--- a/solution.py
+++ b/solution.py
@@ -24,12 +24,12 @@
 F32 = jnp.float32
 BF16 = jnp.bfloat16
 MESH = pl.DeviceIdType.MESH
-QR = 112
+QR = 96
 PH = 32
 TOKEN_BLOCK = 128
 NBLOCK = CROP // TOKEN_BLOCK
 
-SENDS = 200
+SENDS = 256
 
 
 def dot(a, b, dims=((1,), (0,))):
@@ -39,7 +39,7 @@
 def kernel(
     grad_hbm, ctx_hbm, res_hbm, gain_ref, codes_hbm, exp_hbm, down_hbm, up_hbm, map_hbm, len_ref,
     cg_out, hg_out, dg_out, ug_out, fh_out,
-    W, C, DX, DN, SLAB, WS, WT, WX, GI, GM, A1, A2, A3, ACC, HX, PART, RS, RR, LR, ST, SX, SZ, TX, TZ,
+    W, C, DX, DN, SLAB, WS, WT, WX, GI, GM, A1, A2, AM, A3, ACC, HX, PART, RS, RR, LR, ST, SX, SZ, TX, TZ,
     UA, UC, UY, DA, DC, DY, GS, RES, EXP, DIN, UP, MAP, CG, HG, DG, UG, FH,
     send_sem, recv_sem, load_sem,
 ):
@@ -137,7 +137,7 @@
         return start(right), start(left)
 
     def qz(step):
-        return z_ring(step, x, 0, 64, QR)
+        return z_ring(step, x, 0, 48, QR)
 
     def pz(step, column):
         return z_ring(step, column, QR, QR + PH, ROWS)
@@ -160,7 +160,7 @@
     def q_second(*places):
         for rz in places:
             arrived(qx1[rz])
-            qx2[rz] = x_second(rz, 0, 64 if rz % 2 == 0 else 48, QR)
+            qx2[rz] = x_second(rz, 0, 48, QR)
 
     def p_next(step, column, name):
         if step > 1:
@@ -203,6 +203,15 @@
     for r in range(1, NX):
         wx.append(start(copy(WS.at[lax.rem(x + r, NX), core], WX.at[NX - r, y, core], dev_x(r))))
 
+    load_grad.wait()
+    for i in range(32):
+        g = GI[:, i * COLS : (i + 1) * COLS].astype(F32)
+        last = [g[4 * q : 4 * q + 4, 256:COLS] for q in range(3)]
+        side = jnp.concatenate(last + [jnp.zeros((4, 64), F32)], axis=1)
+        GM[i % NX, i // NX] = jnp.concatenate([g[:, 0:256], side], axis=0).astype(BF16)
+    gx = [start(copy(GM.at[lax.rem(x + r, NX)], A1.at[x], dev_x(r))) for r in range(1, NX)]
+    A1[x] = GM[x]
+
     arrived(qz_c[1])
     qz_c[2] = qz(2)
     q_first(1, 7)
@@ -214,14 +223,19 @@
     def y_unit(rel):
         return WX.at[1:NX, lax.rem(y + rel, NY), core]
 
+    y_c = {}
+
     def y_ring(step):
-        if step < 4:
-            a = y_unit(NY - step + 1)
-            b = y_unit(step - 1)
-        else:
-            a = WX.at[1:NX, lax.rem(y + 5, NY), core, 0:48]
-            b = WX.at[1:NX, lax.rem(y + 3, NY), core, 48:80]
-        return start(copy(a, a, dev_y(1))), start(copy(b, b, dev_y(NY - 1)))
+        for r in range(1, NX):
+            if step > 1:
+                arrived(y_c[r, step - 1])
+            if step < 4:
+                a = WX.at[r, lax.rem(y + NY - step + 1, NY), core]
+                b = WX.at[r, lax.rem(y + step - 1, NY), core]
+            else:
+                a = WX.at[r, lax.rem(y + 5, NY), core, 0:48]
+                b = WX.at[r, lax.rem(y + 3, NY), core, 48:80]
+            y_c[r, step] = (start(copy(a, a, dev_y(1))), start(copy(b, b, dev_y(NY - 1))))
 
     swaps = []
 
@@ -232,21 +246,16 @@
 
     for c in wx:
         c.wait_recv()
-    y1 = y_ring(1)
+    y_ring(1)
     core_swap(0)
     for c in dx:
         c.wait_recv()
     DN[0] = jnp.concatenate([DX[i, :, 0:ROWS] for i in range(NX)], axis=1)
     dn1 = dn_ring(1)
-
-    load_grad.wait()
-    for i in range(32):
-        g = GI[:, i * COLS : (i + 1) * COLS].astype(F32)
-        last = [g[4 * q : 4 * q + 4, 256:COLS] for q in range(3)]
-        side = jnp.concatenate(last + [jnp.zeros((4, 64), F32)], axis=1)
-        GM[i % NX, i // NX] = jnp.concatenate([g[:, 0:256], side], axis=0).astype(BF16)
-    gx = [start(copy(GM.at[lax.rem(x + r, NX)], A1.at[x], dev_x(r))) for r in range(1, NX)]
-    A1[x] = GM[x]
+    for c in gx:
+        c.wait_recv()
+    A2[z] = A1[:, z]
+    gz = [start(copy(A1.at[:, lax.rem(z + r, NZ)], A2.at[z], dev_z(r))) for r in range(1, NZ)]
 
     for b in range(DIMS // BLKR):
         lanes = slice(b * BLKR, (b + 1) * BLKR)
@@ -258,11 +267,13 @@
     q_first(2, 6)
     arrived(px2)
     p_next(1, opposite, "opposite")
-
-    for c in gx:
-        c.wait_recv()
-    A2[z] = A1[:, z]
-    gz = [start(copy(A1.at[:, lax.rem(z + r, NZ)], A2.at[z], dev_z(r))) for r in range(1, NZ)]
+    for c in gz:
+        c.wait_recv()
+    away = (1 - sec) * (NZ // 2)
+    am = (
+        start(copy(A2.at[pl.ds(away, 2)], AM.at[0], dev_y(2))),
+        start(copy(A2.at[pl.ds(away + 2, 2)], AM.at[1], dev_y(NY - 2))),
+    )
 
     q_second(1, 7)
     p_next(2, before, "before")
@@ -270,6 +281,10 @@
     p_next(3, x, "own")
     arrived(dn1)
     dn2 = dn_ring(2)
+    y_ring(2)
+    core_swap(1, 7)
+    arrived(am)
+    ga = (start(copy(AM.at[0], A3.at[0:2], dev_y(2))), start(copy(AM.at[1], A3.at[2:4], dev_y(NY - 2))))
 
     def turn(k):
         WT[...] = W[0:COLS, pl.ds(pl.multiple_of(k * group + x * BLKR, BLKR), 256)].T
@@ -287,11 +302,10 @@
     p_next(4, x, "own")
     arrived(dn2)
     dn3 = dn_ring(3)
+    y_ring(3)
+    core_swap(2, 6)
     for k in range(NZ // 2):
         turn(k)
-    arrived(y1)
-    y2 = y_ring(2)
-    core_swap(1, 7)
 
     arrived(qz_c[4])
     q_first(4)
@@ -301,9 +315,8 @@
     p_next(4, after, "after")
     arrived(dn3)
     dn4 = dn_ring(4)
-    for c in gz:
-        c.wait_recv()
-    ga = start(copy(A2.at[pl.ds((1 - sec) * (NZ // 2), NZ // 2)], A3, (dp, t, 1 - sec)))
+    y_ring(4)
+    core_swap(3, 5)
     for k in range(NZ // 2, NZ):
         turn(k)
 
@@ -321,15 +334,12 @@
     q_second(4)
     p_next(4, opposite, "opposite")
     forward(0)
-    arrived(y2)
-    y3 = y_ring(3)
-    core_swap(2, 6)
     forward(1)
     forward(7)
 
     for c in load_rest:
         c.wait()
-    ga.wait_recv()
+    arrived(ga)
     residue = MAP[...]
     block = lax.shift_right_logical(residue * 43691, 19)
     row = residue - block * OWNED
@@ -354,9 +364,6 @@
     forward(6)
     forward(3)
     forward(5)
-    arrived(y3)
-    y4 = y_ring(4)
-    core_swap(3, 5)
     arrived(dn4)
     forward(4)
 
@@ -371,7 +378,8 @@
         c.wait_recv()
     SZ[0] = (ST[...] + SX[1]) + (SX[2] + SX[3])
     sz = [start(copy(SZ.at[0], SZ.at[r], dev_z(r))) for r in range(1, NZ)]
-    arrived(y4)
+    for r in range(1, NX):
+        arrived(y_c[r, 4])
     core_swap(4)
     for c in sz:
         c.wait_recv()
@@ -461,6 +469,37 @@
             left = copy(RS.at[b, 1, step - 1], LR.at[b, step - 1], dev_z(NZ - 1))
         rs[b, step] = (start(right), start(left))
 
+    def rs_short(b, step):
+        if step == 1:
+            for side, three in ((0, 3), (1, 5)):
+                lo, hi = (0, HALF) if side == 0 else (HALF, ROWS)
+                RS[b, side, 0, 0:HALF] = part(b, 4)[lo:hi].astype(BF16)
+                RS[b, side, 1] = part(b, three).astype(BF16)
+            rs[b, 1] = (
+                start(copy(RS.at[b, 0, 0, 0:HALF], RR.at[b, 0, 0:HALF], dev_z(2))),
+                start(copy(RS.at[b, 1, 0, 0:HALF], LR.at[b, 0, 0:HALF], dev_z(NZ - 2))),
+                start(copy(RS.at[b, 0, 1], RR.at[b, 1], dev_z(1))),
+                start(copy(RS.at[b, 1, 1], LR.at[b, 1], dev_z(NZ - 1))),
+            )
+            RS[b, 0, 2] = part(b, 1).astype(BF16)
+            RS[b, 1, 2] = part(b, 7).astype(BF16)
+            rs[b, 4] = (
+                start(copy(RS.at[b, 0, 2], RR.at[b, 2], dev_z(1))),
+                start(copy(RS.at[b, 1, 2], LR.at[b, 2], dev_z(NZ - 1))),
+            )
+        else:
+            arrived(rs[b, 1])
+            right = part(b, 2) + RR[b, 1].astype(F32)
+            left = part(b, 6) + LR[b, 1].astype(F32)
+            RS[b, 0, 3, 0:HALF] = (right[0:HALF] + RR[b, 0, 0:HALF].astype(F32)).astype(BF16)
+            RS[b, 0, 3, HALF:ROWS] = right[HALF:ROWS].astype(BF16)
+            RS[b, 1, 3, 0:HALF] = left[0:HALF].astype(BF16)
+            RS[b, 1, 3, HALF:ROWS] = (left[HALF:ROWS] + LR[b, 0, 0:HALF].astype(F32)).astype(BF16)
+            rs[b, 4] += (
+                start(copy(RS.at[b, 0, 3], RR.at[b, 3], dev_z(2))),
+                start(copy(RS.at[b, 1, 3], LR.at[b, 3], dev_z(NZ - 2))),
+            )
+
     partials(0)
     rs_step(0, 1)
     h2.append(hx_second(2))
@@ -479,25 +518,25 @@
     rs_step(0, 3)
     rs_step(1, 2)
     partials(2)
-    rs_step(2, 1)
+    rs_short(2, 1)
     rs_step(0, 4)
     rs_step(1, 3)
-    rs_step(2, 2)
+    rs_short(2, 2)
     rs_step(1, 4)
     for c in uy:
         c.wait_recv()
     UG[...] = jnp.sum(UY[...], axis=0)
     out_ug = local_copy(UG, ug_out)
-    rs_step(2, 3)
     for c in dy:
         c.wait_recv()
     DG[...] = jnp.sum(DY[...], axis=0)
     out_dg = local_copy(DG, dg_out)
-    rs_step(2, 4)
     for b in range(NBLOCK):
         arrived(rs[b, 4])
         lanes = slice(b * TOKEN_BLOCK, (b + 1) * TOKEN_BLOCK)
         total = part(b, 0) + RR[b, 3].astype(F32) + LR[b, 3].astype(F32)
+        if b == NBLOCK - 1:
+            total = total + RR[b, 2].astype(F32) + LR[b, 2].astype(F32)
         CG[:, lanes] = (total + adapter[:, lanes]).astype(BF16)
     out_cg = local_copy(CG, cg_out)
 
@@ -509,8 +548,16 @@
 
 
 def finish(*refs):
-    for array, out in zip(refs[:5], refs[5:]):
-        out[...] = array[...]
+    arrays, outs, held, sems = refs[:5], refs[5:10], refs[10:15], refs[15]
+    loads = [pltpu.make_async_copy(a, h, sems.at[0, i]) for i, (a, h) in enumerate(zip(arrays, held))]
+    stores = [pltpu.make_async_copy(h, o, sems.at[1, i]) for i, (h, o) in enumerate(zip(held, outs))]
+    for c in loads:
+        c.start()
+    for load, store in zip(loads, stores):
+        load.wait()
+        store.start()
+    for c in stores:
+        c.wait()
 
 
 def on_device(grad, context, residual, gain, codes, exponents, down, up, residue_map, lengths):
@@ -541,6 +588,7 @@
             pltpu.VMEM((NX, NZ, SLOT, 256), BF16),
             pltpu.VMEM((NX, NZ, SLOT, 256), BF16),
             pltpu.VMEM((NZ, NX, SLOT, 256), BF16),
+            pltpu.VMEM((2, 2, NX, SLOT, 256), BF16),
             pltpu.VMEM((NZ // 2, NX, SLOT, 256), BF16),
             pltpu.VMEM((COLS + RANK, CROP), F32),
             pltpu.VMEM((NBLOCK, NX, COLS, TOKEN_BLOCK), BF16),
@@ -582,8 +630,9 @@
     cg, hg, dg, ug, fh = pl.pallas_call(
         finish,
         out_shape=shapes,
-        in_specs=[vmem] * 5,
-        out_specs=[vmem] * 5,
+        in_specs=[anywhere] * 5,
+        out_specs=[anywhere] * 5,
+        scratch_shapes=[pltpu.VMEM(a.shape, a.dtype) for a in shapes] + [pltpu.SemaphoreType.DMA((2, 5))],
     )(*results)
     return cg, hg.T, dg.T, ug, fh.T
 

time: 108 us -> 98.9 us (0.916)
  Pallas kernels: 106 us -> 97.3 us
    pallas_call x1, Pallas kernels: 104 us -> 95.4 us  [on_device(): pl.pallas_call(kernel, out_shape=shapes, in_specs=[anywhere] * 3 + [vmem]...]
where the time goes in v3:
time: 98.9 us; the launch traced here: 98.6 us
  Pallas kernels  97.3 us (98%)
  between operations  1.29 us (1%)
    pallas_call x1, Pallas kernels, on_device(): pl.pallas_call(kernel, out_shape=shapes, in_specs=[anywhere] * 3 + [vmem]...  95.4 us

profile of v3, /device:TPU:6, one launch (start us, length us, event | category | flops | bytes accessed | tf_op | source)
XLA Modules:
  0.0 98.6 jit_solution(11637055405267107379)
XLA Ops:
  1.3 95.4 %shard_map.137 = (bf16[160,384]{1,0:T(8,128)(2,1)}, bf16[320,384]{1,0:T(8,128)(2,1)}, f32[16,160]{1,0:T(8,128)}, f32[16,320]{1,0:T(8,128)}, bf16[320,384]{1,0:T(8,128)(2,1)}) custom-call(bf16[12,10240]{1,0:T(8,128)(2,1)} %grad_hbm.1, bf16[160,384]{1,0:T(8,128)(2,1)} %bitcast.12, bf16[320,384]{1,0:T(8,128)(2,1)} %bitcast.9, bf16[320]{0:T(512)(128)(2,1)} %gain_ref.1, ...), custom_call_target="tpu_custom_call" | custom-call | flops 2516582400 | bytes 8388608 | tf_op jit(solution)/shard_map/pallas_call | solution.py:573
  96.7 1.9 %shard_map.138 = (bf16[160,384]{1,0:T(8,128)(2,1)}, bf16[320,384]{1,0:T(8,128)(2,1)}, f32[16,160]{1,0:T(8,128)}, f32[16,320]{1,0:T(8,128)}, bf16[320,384]{1,0:T(8,128)(2,1)}) custom-call(bf16[160,384]{1,0:T(8,128)(2,1)} %get-tuple-element.15.refs_0_, bf16[320,384]{1,0:T(8,128)(2,1)} %get-tuple-element.16.refs_1_, f32[16,160]{1,0:T(8,128)} %get-tuple-element.17.refs_2_, ...), custom_call_target="tpu_custom_call" | custom-call | tf_op jit(solution)/shard_map/pallas_call | solution.py:630

commit v4 on v3

--- a/solution.py
+++ b/solution.py
@@ -407,27 +407,27 @@
             start(copy(HX.at[b, 1, 160:COLS], HX.at[b, 2, 160:COLS], dev_x(NX - 1))),
         )
 
-    h1 = [hx_first(0)]
-    TX[0] = dot(UP[...], gradient)
+    h1 = [hx_first(0), hx_first(1)]
+    TX[0] = dot(UP[...], gradient).astype(BF16)
     tx = [start(copy(TX.at[0], TX.at[r], dev_x(r))) for r in range(1, NX)]
-    h1 += [hx_first(1), hx_first(2)]
+    UA[...] = ADAPTER_SCALE * dot(inner, gradient, ((1,), (1,)))
+    uc = start(copy(UA, UC, other_core))
     HG[...] = gradient
     out_hg = local_copy(HG, hg_out)
     FH[...] = (gain * normed).astype(BF16)
     out_fh = local_copy(FH, fh_out)
-    UA[...] = ADAPTER_SCALE * dot(inner, gradient, ((1,), (1,)))
-    uc = start(copy(UA, UC, other_core))
+    h2 = [hx_second(0)]
+    h1.append(hx_first(2))
     for c in tx:
         c.wait_recv()
-    TZ[0] = (TX[0] + TX[1]) + (TX[2] + TX[3])
+    TZ[0] = jnp.sum(TX[...].astype(F32), axis=0).astype(BF16)
     tz = [start(copy(TZ.at[0], TZ.at[r], dev_z(r))) for r in range(1, NZ)]
-    h2 = [hx_second(0)]
     uc.wait_recv()
     UY[0] = UA[...] + UC[...]
     uy = [start(copy(UY.at[0], UY.at[r], dev_y(r))) for r in range(1, NY)]
+    h2.append(hx_second(1))
     for c in swaps:
         c.wait_recv()
-    h2.append(hx_second(1))
 
     halves = NZ * ROWS // 2
 
@@ -449,27 +449,6 @@
     rs = {}
 
     def rs_step(b, step):
-        if step == 1:
-            RS[b, 0, 0, 0:HALF] = part(b, 4)[0:HALF].astype(BF16)
-            RS[b, 1, 0, 0:HALF] = part(b, 4)[HALF:ROWS].astype(BF16)
-            right = copy(RS.at[b, 0, 0, 0:HALF], RR.at[b, 0, 0:HALF], dev_z(1))
-            left = copy(RS.at[b, 1, 0, 0:HALF], LR.at[b, 0, 0:HALF], dev_z(NZ - 1))
-        else:
-            arrived(rs[b, step - 1])
-            mine_right, mine_left = part(b, 5 - step), part(b, 3 + step)
-            if step == 2:
-                RS[b, 0, 1, 0:HALF] = (mine_right[0:HALF] + RR[b, 0, 0:HALF].astype(F32)).astype(BF16)
-                RS[b, 0, 1, HALF:ROWS] = mine_right[HALF:ROWS].astype(BF16)
-                RS[b, 1, 1, 0:HALF] = mine_left[0:HALF].astype(BF16)
-                RS[b, 1, 1, HALF:ROWS] = (mine_left[HALF:ROWS] + LR[b, 0, 0:HALF].astype(F32)).astype(BF16)
-            else:
-                RS[b, 0, step - 1] = (mine_right + RR[b, step - 2].astype(F32)).astype(BF16)
-                RS[b, 1, step - 1] = (mine_left + LR[b, step - 2].astype(F32)).astype(BF16)
-            right = copy(RS.at[b, 0, step - 1], RR.at[b, step - 1], dev_z(1))
-            left = copy(RS.at[b, 1, step - 1], LR.at[b, step - 1], dev_z(NZ - 1))
-        rs[b, step] = (start(right), start(left))
-
-    def rs_short(b, step):
         if step == 1:
             for side, three in ((0, 3), (1, 5)):
                 lo, hi = (0, HALF) if side == 0 else (HALF, ROWS)
@@ -503,26 +482,22 @@
     partials(0)
     rs_step(0, 1)
     h2.append(hx_second(2))
+    partials(1)
+    rs_step(1, 1)
     for c in tz:
         c.wait_recv()
-    through_all = jnp.sum(TZ[...], axis=0).astype(BF16)
+    through_all = jnp.sum(TZ[...].astype(F32), axis=0).astype(BF16)
     DA[...] = ADAPTER_SCALE * dot(through_all, C[x], ((1,), (1,)))
     dc = start(copy(DA, DC, other_core))
-    adapter = ADAPTER_SCALE * dot(DIN[...], through_all, ((0,), (0,)))
     rs_step(0, 2)
-    partials(1)
-    rs_step(1, 1)
+    partials(2)
+    rs_step(2, 1)
     dc.wait_recv()
     DY[0] = DA[...] + DC[...]
     dy = [start(copy(DY.at[0], DY.at[r], dev_y(r))) for r in range(1, NY)]
-    rs_step(0, 3)
+    adapter = ADAPTER_SCALE * dot(DIN[...], through_all, ((0,), (0,)))
     rs_step(1, 2)
-    partials(2)
-    rs_short(2, 1)
-    rs_step(0, 4)
-    rs_step(1, 3)
-    rs_short(2, 2)
-    rs_step(1, 4)
+    rs_step(2, 2)
     for c in uy:
         c.wait_recv()
     UG[...] = jnp.sum(UY[...], axis=0)
@@ -534,9 +509,8 @@
     for b in range(NBLOCK):
         arrived(rs[b, 4])
         lanes = slice(b * TOKEN_BLOCK, (b + 1) * TOKEN_BLOCK)
-        total = part(b, 0) + RR[b, 3].astype(F32) + LR[b, 3].astype(F32)
-        if b == NBLOCK - 1:
-            total = total + RR[b, 2].astype(F32) + LR[b, 2].astype(F32)
+        total = part(b, 0) + (RR[b, 2].astype(F32) + LR[b, 2].astype(F32))
+        total = total + (RR[b, 3].astype(F32) + LR[b, 3].astype(F32))
         CG[:, lanes] = (total + adapter[:, lanes]).astype(BF16)
     out_cg = local_copy(CG, cg_out)
 
@@ -599,8 +573,8 @@
             pltpu.VMEM((4, CROP), F32),
             pltpu.VMEM((NX, 4, CROP), F32),
             pltpu.VMEM((NZ, 4, CROP), F32),
-            pltpu.VMEM((NX, RANK, CROP), F32),
-            pltpu.VMEM((NZ, RANK, CROP), F32),
+            pltpu.VMEM((NX, RANK, CROP), BF16),
+            pltpu.VMEM((NZ, RANK, CROP), BF16),
             pltpu.VMEM((RANK, COLS), F32),
             pltpu.VMEM((RANK, COLS), F32),
             pltpu.VMEM((NY, RANK, COLS), F32),

time: 98.9 us -> 93.1 us (0.941)
  Pallas kernels: 97.3 us -> 90.9 us
    pallas_call x1, Pallas kernels: 95.4 us -> 88.9 us  [on_device(): pl.pallas_call(kernel, out_shape=shapes, in_specs=[anywhere] * 3 + [vmem]...]
where the time goes in v4:
time: 93.1 us; the launch traced here: 92.2 us
  Pallas kernels  90.9 us (98%)
  between operations  1.29 us (1%)
    pallas_call x1, Pallas kernels, on_device(): pl.pallas_call(kernel, out_shape=shapes, in_specs=[anywhere] * 3 + [vmem]...  88.9 us
    pallas_call x1, Pallas kernels, on_device(): pl.pallas_call(finish, out_shape=shapes, in_specs=[anywhere] * 5, out_spe...  1.93 us

profile of v4, /device:TPU:6, one launch (start us, length us, event | category | flops | bytes accessed | tf_op | source)
XLA Modules:
  0.0 92.2 jit_solution(18322059445889476765)
XLA Ops:
  1.3 88.9 %shard_map.137 = (bf16[160,384]{1,0:T(8,128)(2,1)}, bf16[320,384]{1,0:T(8,128)(2,1)}, f32[16,160]{1,0:T(8,128)}, f32[16,320]{1,0:T(8,128)}, bf16[320,384]{1,0:T(8,128)(2,1)}) custom-call(bf16[12,10240]{1,0:T(8,128)(2,1)} %grad_hbm.1, bf16[160,384]{1,0:T(8,128)(2,1)} %bitcast.12, bf16[320,384]{1,0:T(8,128)(2,1)} %bitcast.9, bf16[320]{0:T(512)(128)(2,1)} %gain_ref.1, ...), custom_call_target="tpu_custom_call" | custom-call | flops 2516582400 | bytes 8388608 | tf_op jit(solution)/shard_map/pallas_call | solution.py:547
  90.2 1.9 %shard_map.138 = (bf16[160,384]{1,0:T(8,128)(2,1)}, bf16[320,384]{1,0:T(8,128)(2,1)}, f32[16,160]{1,0:T(8,128)}, f32[16,320]{1,0:T(8,128)}, bf16[320,384]{1,0:T(8,128)(2,1)}) custom-call(bf16[160,384]{1,0:T(8,128)(2,1)} %get-tuple-element.15.refs_0_, bf16[320,384]{1,0:T(8,128)(2,1)} %get-tuple-element.16.refs_1_, f32[16,160]{1,0:T(8,128)} %get-tuple-element.17.refs_2_, ...), custom_call_target="tpu_custom_call" | custom-call | tf_op jit(solution)/shard_map/pallas_call | solution.py:604

commit v5 on v4

--- a/solution.py
+++ b/solution.py
@@ -119,6 +119,11 @@
         for c in pair:
             c.wait_recv()
 
+    def drain(count):
+        for c in pending[:count]:
+            c.wait_send()
+        del pending[:count]
+
     load_down.wait()
     DX[x] = jnp.concatenate([DIN[...], jnp.zeros((RANK, 96), BF16)], axis=1)
     load_ctx.wait()
@@ -307,6 +312,7 @@
     for k in range(NZ // 2):
         turn(k)
 
+    early = len(pending)
     arrived(qz_c[4])
     q_first(4)
     p_next(3, opposite, "opposite")
@@ -367,6 +373,7 @@
     arrived(dn4)
     forward(4)
 
+    gathered = len(pending) - early
     inner = ACC[COLS : COLS + RANK, :].astype(BF16)
     hidden = ACC[0:COLS, :] + ADAPTER_SCALE * dot(UP[...], inner, ((0,), (0,))) + RES[...].astype(F32)
     ST[0:1, :] = jnp.sum(hidden, axis=0, keepdims=True)
@@ -381,6 +388,7 @@
     for r in range(1, NX):
         arrived(y_c[r, 4])
     core_swap(4)
+    drain(early)
     for c in sz:
         c.wait_recv()
     sums = jnp.sum(SZ[...], axis=0) / MODEL_WIDTH
@@ -389,10 +397,13 @@
     inverse = lax.rsqrt(variance + 1e-05)
     first_mean = sums[2:3, :]
     second_mean = inverse * (sums[3:4, :] - average * first_mean)
-    normed = (hidden - average) * inverse
-    gradient = (inverse * (scaled - first_mean - normed * second_mean)).astype(BF16)
-    for b in range(NBLOCK):
-        HX[b, 0] = gradient[:, b * TOKEN_BLOCK : (b + 1) * TOKEN_BLOCK]
+
+    def norm(b):
+        lanes = slice(b * TOKEN_BLOCK, (b + 1) * TOKEN_BLOCK)
+        normed = (hidden[:, lanes] - average[:, lanes]) * inverse[:, lanes]
+        rest = scaled[:, lanes] - first_mean[:, lanes] - normed * second_mean[:, lanes]
+        HX[b, 0] = (inverse[:, lanes] * rest).astype(BF16)
+        FH[:, lanes] = (gain * normed).astype(BF16)
 
     def hx_first(b):
         return (
@@ -407,14 +418,18 @@
             start(copy(HX.at[b, 1, 160:COLS], HX.at[b, 2, 160:COLS], dev_x(NX - 1))),
         )
 
-    h1 = [hx_first(0), hx_first(1)]
+    h1 = []
+    for b in range(NBLOCK):
+        norm(b)
+        if b < 2:
+            h1.append(hx_first(b))
+    gradient = jnp.concatenate([HX[b, 0] for b in range(NBLOCK)], axis=1)
     TX[0] = dot(UP[...], gradient).astype(BF16)
     tx = [start(copy(TX.at[0], TX.at[r], dev_x(r))) for r in range(1, NX)]
     UA[...] = ADAPTER_SCALE * dot(inner, gradient, ((1,), (1,)))
     uc = start(copy(UA, UC, other_core))
     HG[...] = gradient
     out_hg = local_copy(HG, hg_out)
-    FH[...] = (gain * normed).astype(BF16)
     out_fh = local_copy(FH, fh_out)
     h2 = [hx_second(0)]
     h1.append(hx_first(2))
@@ -426,8 +441,10 @@
     UY[0] = UA[...] + UC[...]
     uy = [start(copy(UY.at[0], UY.at[r], dev_y(r))) for r in range(1, NY)]
     h2.append(hx_second(1))
+    drain(gathered)
     for c in swaps:
         c.wait_recv()
+    exchanged = len(pending)
 
     halves = NZ * ROWS // 2
 
@@ -498,6 +515,7 @@
     adapter = ADAPTER_SCALE * dot(DIN[...], through_all, ((0,), (0,)))
     rs_step(1, 2)
     rs_step(2, 2)
+    drain(exchanged)
     for c in uy:
         c.wait_recv()
     UG[...] = jnp.sum(UY[...], axis=0)
@@ -514,9 +532,7 @@
         CG[:, lanes] = (total + adapter[:, lanes]).astype(BF16)
     out_cg = local_copy(CG, cg_out)
 
-    for c in pending:
-        c.wait_send()
-
+    drain(len(pending))
     for c in (out_hg, out_fh, out_ug, out_dg, out_cg):
         c.wait()
 

time: 93.1 us -> 92.8 us (level)
  no operation moved by 1% of the time
where the time goes in v5:
time: 92.8 us; the launch traced here: 92.6 us
  Pallas kernels  91.3 us (98%)
  between operations  1.29 us (1%)
    pallas_call x1, Pallas kernels, on_device(): pl.pallas_call(kernel, out_shape=shapes, in_specs=[anywhere] * 3 + [vmem]...  89.4 us
    pallas_call x1, Pallas kernels, on_device(): pl.pallas_call(finish, out_shape=shapes, in_specs=[anywhere] * 5, out_spe...  1.93 us

profile of v5, /device:TPU:6, one launch (start us, length us, event | category | flops | bytes accessed | tf_op | source)
XLA Modules:
  0.0 92.6 jit_solution(15746006090828710347)
XLA Ops:
  1.3 89.4 %shard_map.137 = (bf16[160,384]{1,0:T(8,128)(2,1)}, bf16[320,384]{1,0:T(8,128)(2,1)}, f32[16,160]{1,0:T(8,128)}, f32[16,320]{1,0:T(8,128)}, bf16[320,384]{1,0:T(8,128)(2,1)}) custom-call(bf16[12,10240]{1,0:T(8,128)(2,1)} %grad_hbm.1, bf16[160,384]{1,0:T(8,128)(2,1)} %bitcast.12, bf16[320,384]{1,0:T(8,128)(2,1)} %bitcast.9, bf16[320]{0:T(512)(128)(2,1)} %gain_ref.1, ...), custom_call_target="tpu_custom_call" | custom-call | flops 2516582400 | bytes 8388608 | tf_op jit(solution)/shard_map/pallas_call | solution.py:563
  90.7 1.9 %shard_map.138 = (bf16[160,384]{1,0:T(8,128)(2,1)}, bf16[320,384]{1,0:T(8,128)(2,1)}, f32[16,160]{1,0:T(8,128)}, f32[16,320]{1,0:T(8,128)}, bf16[320,384]{1,0:T(8,128)(2,1)}) custom-call(bf16[160,384]{1,0:T(8,128)(2,1)} %get-tuple-element.15.refs_0_, bf16[320,384]{1,0:T(8,128)(2,1)} %get-tuple-element.16.refs_1_, f32[16,160]{1,0:T(8,128)} %get-tuple-element.17.refs_2_, ...), custom_call_target="tpu_custom_call" | custom-call | tf_op jit(solution)/shard_map/pallas_call | solution.py:620
